TPU v7x, 128 devices: a whole 4x4x4 slice. The times are simulated.
128 devices in a mesh: roll: 16 (over z, y_hi, core), kvh: 8 (over y_lo, x).
Axes of the slice: x: 4, y: 4 (y_hi: 2, y_lo: 2; y = y_hi * 2 + y_lo), z: 4, core: 2. Of those that a mesh axis runs over, the one named last changes fastest.
Arguments:
- out_grad: bfloat16 [16, 256, 5120], P('roll', 'kvh'), may hold values from -48 to 48
- out_weight: bfloat16 [8, 5, 128, 5120], P('kvh'), may hold values from -0.078125 to 0.078125
- queries: bfloat16 [16, 256, 8, 5, 128], P('roll', None, 'kvh'), may hold values from -16 to 16
- keys_new: bfloat16 [16, 256, 8, 128], P('roll', None, 'kvh'), may hold values from -16 to 16
- values_new: bfloat16 [16, 256, 8, 128], P('roll', None, 'kvh'), may hold values from -6 to 6
- keys_prompt: bfloat16 [4096, 8, 128], P('roll', 'kvh'), may hold values from -6 to 6
- values_prompt: bfloat16 [4096, 8, 128], P('roll', 'kvh'), may hold values from -6 to 6
- offsets: int32 [16], P('roll'), may hold values from 0 to 3840
Outputs:
- grad_queries: bfloat16 [16, 256, 8, 5, 128], P('roll', None, 'kvh')
- grad_keys_new: bfloat16 [16, 256, 8, 128], P('roll', None, 'kvh')
- grad_values_new: bfloat16 [16, 256, 8, 128], P('roll', None, 'kvh')
- grad_keys_prompt: bfloat16 [4096, 8, 128], P('roll', 'kvh')
- grad_values_prompt: bfloat16 [4096, 8, 128], P('roll', 'kvh')
Inputs may be any that keep to these rules, and one draw needn't show every extreme that they name: `offsets`: each slice lies inside a response of 4096 tokens.
All inputs are finite; a program needn't handle non-finite values.
Results may differ from a plain program's by a relative error of at most 0.015.
The roundings to bfloat16 on the way count: a program that leaves them out, or rounds other values in their place, can miss the bound.
Values may be sent and summed in bfloat16 or wider, within the bound.
A program may use at most 64 MiB of HBM per device.

v0:
```python
import math

import jax
import jax.numpy as jnp
from jax import lax
from jax.sharding import PartitionSpec as P

theta_base = 1000000.0


def rotation(positions, head_width):
    half_width = head_width // 2
    frequency = jnp.power(theta_base, -(jnp.arange(half_width, dtype=jnp.float32) / half_width))
    angles = positions.astype(jnp.float32)[:, None] * frequency[None, :]
    return (jnp.cos(angles), jnp.sin(angles))


def rotate(vectors, cos_part, sin_part, direction):
    half_width = vectors.shape[-1] // 2
    front_half = vectors[..., :half_width]
    back_half = vectors[..., half_width:]
    return jnp.concatenate(
        [
            front_half * cos_part - direction * back_half * sin_part,
            back_half * cos_part + direction * front_half * sin_part,
        ],
        axis=-1,
    )


def inner_dot(left, right):
    return lax.dot_general(
        left, right, (((1,), (1,)), ((), ())), preferred_element_type=jnp.float32
    )


def outer_sum(left, right):
    return lax.dot_general(
        left, right, (((0,), (0,)), ((), ())), preferred_element_type=jnp.float32
    )


def block_grads(context, key_block, value_block):
    query_rows, grad_rows, log_total, row_delta, score_scale = context
    scores = inner_dot(query_rows, key_block) * score_scale
    attn_probs = jnp.exp(scores - log_total[:, None]).astype(jnp.bfloat16)
    prob_grad = inner_dot(grad_rows, value_block)
    score_grad = (
        attn_probs.astype(jnp.float32) * (prob_grad - row_delta[:, None]) * score_scale
    ).astype(jnp.bfloat16)
    return (attn_probs, score_grad)


def local(out_grad, out_weight, queries, keys_new, values_new, keys_prompt, values_prompt, offsets):
    roll_local, seq_len, kv_local, group_size, head_width = queries.shape
    prompt_local = keys_prompt.shape[0]
    prompt_total = prompt_local * lax.axis_size("roll")
    score_scale = head_width ** (-0.5)
    row_total = roll_local * seq_len * group_size
    attn_grad = jnp.einsum(
        "rsc,ghdc->rsghd",
        lax.all_gather(out_grad, "kvh", axis=1, tiled=True),
        out_weight,
        preferred_element_type=jnp.float32,
    ).astype(jnp.bfloat16)
    cached_keys, cached_values = (
        lax.all_gather(keys_prompt, "roll", axis=0, tiled=True),
        lax.all_gather(values_prompt, "roll", axis=0, tiled=True),
    )
    positions = prompt_total + offsets[:, None] + jnp.arange(seq_len, dtype=jnp.int32)[None, :]
    cos_flat, sin_flat = rotation(positions.reshape(-1), head_width)
    cos_four = cos_flat.reshape(roll_local, seq_len, 1, head_width // 2)
    sin_four = sin_flat.reshape(roll_local, seq_len, 1, head_width // 2)
    query_rot = rotate(
        queries.astype(jnp.float32), cos_four[:, :, :, None], sin_four[:, :, :, None], 1.0
    ).astype(jnp.bfloat16)
    key_rot = rotate(keys_new.astype(jnp.float32), cos_four, sin_four, 1.0).astype(jnp.bfloat16)
    block_len = math.gcd(prompt_total, 512)
    block_count = prompt_total // block_len
    causal = (jnp.arange(seq_len)[None, :] <= jnp.arange(seq_len)[:, None])[None, :, None, :]
    contexts = []
    query_head = query_rot[:, :, 0]
    key_head = key_rot[:, :, 0]
    value_head = values_new[:, :, 0]
    grad_head = attn_grad[:, :, 0]
    query_rows = query_head.reshape(row_total, head_width)
    grad_rows = grad_head.reshape(row_total, head_width)
    key_blocks = cached_keys[:, 0].reshape(block_count, block_len, head_width)
    value_blocks = cached_values[:, 0].reshape(block_count, block_len, head_width)
    near_scores = (
        jnp.einsum("rshd,rtd->rsht", query_head, key_head, preferred_element_type=jnp.float32)
        * score_scale
    )
    near_scores = jnp.where(causal, near_scores, -jnp.inf)
    near_max = jnp.max(near_scores, axis=3, keepdims=True)
    near_sum = jnp.sum(jnp.exp(near_scores - near_max), axis=3)

    def stat_step(running, key_block):
        old_max, old_sum = running
        scores = inner_dot(query_rows, key_block) * score_scale
        new_max = jnp.maximum(old_max, jnp.max(scores, axis=1))
        new_sum = old_sum * jnp.exp(old_max - new_max) + jnp.sum(
            jnp.exp(scores - new_max[:, None]), axis=1
        )
        return ((new_max, new_sum), None)

    stats, unused = lax.scan(
        stat_step, (near_max.reshape(row_total), near_sum.reshape(row_total)), key_blocks
    )
    log_total = stats[0] + jnp.log(stats[1])
    log_shaped = log_total.reshape(roll_local, seq_len, group_size, 1)
    near_probs = jnp.where(causal, jnp.exp(near_scores - log_shaped), 0.0).astype(jnp.bfloat16)
    near_output = jnp.einsum(
        "rsht,rtd->rshd", near_probs, value_head, preferred_element_type=jnp.float32
    ).reshape(row_total, head_width)

    def output_step(total_out, blocks):
        scores = inner_dot(query_rows, blocks[0]) * score_scale
        attn_probs = jnp.exp(scores - log_total[:, None]).astype(jnp.bfloat16)
        return (
            total_out + jnp.dot(attn_probs, blocks[1], preferred_element_type=jnp.float32),
            None,
        )

    output, unused = lax.scan(output_step, near_output, (key_blocks, value_blocks))
    row_delta = jnp.sum(grad_rows.astype(jnp.float32) * output, axis=1)
    context = (query_rows, grad_rows, log_total, row_delta, score_scale)
    contexts.append(context)
    near_prob_grad = jnp.einsum(
        "rshd,rtd->rsht", grad_head, value_head, preferred_element_type=jnp.float32
    )
    delta_shaped = row_delta.reshape(roll_local, seq_len, group_size, 1)
    near_grad = (
        near_probs.astype(jnp.float32) * (near_prob_grad - delta_shaped) * score_scale
    ).astype(jnp.bfloat16)
    near_query = jnp.einsum(
        "rsht,rtd->rshd", near_grad, key_head, preferred_element_type=jnp.float32
    )
    key_new_grad = jnp.einsum(
        "rsht,rshd->rtd", near_grad, query_head, preferred_element_type=jnp.float32
    )
    value_new_grad = jnp.einsum(
        "rsht,rshd->rtd", near_probs, grad_head, preferred_element_type=jnp.float32
    )
    zero_rows = jnp.zeros((row_total, head_width), jnp.float32)

    def grad_step(total_grad, blocks):
        attn_probs, score_grad = block_grads(context, blocks[0], blocks[1])
        block_term = jnp.stack(
            [outer_sum(score_grad, query_rows), outer_sum(attn_probs, grad_rows)], axis=1
        )
        return (
            total_grad + jnp.dot(score_grad, blocks[0], preferred_element_type=jnp.float32),
            block_term,
        )

    far_query, block_terms = lax.scan(grad_step, zero_rows, (key_blocks, value_blocks))
    term_list = [block_terms.reshape(prompt_total, 2, head_width)]
    query_grad = far_query.reshape(roll_local, seq_len, group_size, head_width) + near_query
    query_list = [rotate(query_grad, cos_four, sin_four, -1.0).astype(jnp.bfloat16)]
    key_list = [
        rotate(key_new_grad, cos_four[:, :, 0], sin_four[:, :, 0], -1.0).astype(jnp.bfloat16)
    ]
    value_list = [value_new_grad.astype(jnp.bfloat16)]
    reduced = lax.psum_scatter(
        jnp.stack(term_list, axis=1).astype(jnp.bfloat16), "roll", scatter_dimension=0, tiled=True
    ).astype(jnp.float32)
    grad_queries = jnp.stack(query_list, axis=2)
    grad_keys_new = jnp.stack(key_list, axis=2)
    grad_values_new = jnp.stack(value_list, axis=2)
    return (
        grad_queries,
        grad_keys_new,
        grad_values_new,
        reduced[:, :, 0].astype(jnp.bfloat16),
        reduced[:, :, 1].astype(jnp.bfloat16),
    )


def solution(mesh):
    placed = (
        P("roll", "kvh", None),
        P("kvh", None, None, None),
        P("roll", None, "kvh", None, None),
        P("roll", None, "kvh", None),
        P("roll", None, "kvh", None),
        P("roll", "kvh", None),
        P("roll", "kvh", None),
        P("roll"),
    )
    return jax.shard_map(
        local,
        mesh=mesh,
        in_specs=placed,
        out_specs=(
            P("roll", None, "kvh", None, None),
            P("roll", None, "kvh", None),
            P("roll", None, "kvh", None),
            P("roll", "kvh", None),
            P("roll", "kvh", None),
        ),
        check_vma=False,
    )
```

profile of v0, /device:TPU:1, one launch (start us, length us, event | category | flops | bytes accessed | tf_op | source)
XLA Modules:
  0.0 287.3 jit_solution(14173419729338895202)
XLA Ops:
  10.2 0.9 convert_element_type.126
  11.0 0.9 broadcast_multiply_fusion
  12.0 1.2 fusion.70
  13.4 1.0 convert_element_type.124
  15.0 0.9 concatenate.68
  16.2 0.9 concatenate.69
  19.1 40.1 %all-gather.4.cloned.1.call-done = bf16[4096,1,128]{2,0,1:T(8,128)(2,1)} async-done(((bf16[256,1,128]{2,0,1:T(8,128)(2,1)}), bf16[4096,1,128]{2,0,1:T(8,128)(2,1)}) %all-gather.4.cloned.1.call-update) | async-done | bytes 1048592 | tf_op jit(solution)/shard_map/all_gather | solution.py:67
  59.2 15.1 %while.35 = (s32[]{:T(128)}, f32[1280]{0:T(1024)S(1)}, f32[1280]{0:T(1024)S(1)}, bf16[8,512,128]{2,1,0:T(8,128)(2,1)}, bf16[1280,128]{1,0:T(8,128)(2,1)S(1)}, /*index=5*/s32[]{:T(128)}) while((s32[]{:T(128)}, f32[1280]{0:T(1024)S(1)}, f32[1280]{0:T(1024)S(1)}, bf16[8,512,128]{2,1,0:T(8,128)(2,1)}, bf16[1280,128]{1,0:T(8,128)(2,1)S(1)}, ...), condition=%wide.region_5.6_spmd, body=%wide.region_2.5_spmd.sunk | while | flops 170396160 | bytes 5768273 | solution.py:107
  59.2 1.4 fusion.112
  61.0 1.4 fusion.112
  62.9 1.4 fusion.112
  64.8 1.4 fusion.112
  66.7 1.4 fusion.112
  68.6 1.4 fusion.112
  70.5 1.4 fusion.112
  72.3 1.4 fusion.112
  75.2 1.1 dot_general.51
  76.3 1.4 fusion.67
  77.7 27.6 %all-gather.6.cloned.1.call-done = bf16[4096,1,128]{2,0,1:T(8,128)(2,1)} async-done(((bf16[256,1,128]{2,0,1:T(8,128)(2,1)}), bf16[4096,1,128]{2,0,1:T(8,128)(2,1)}) %all-gather.6.cloned.1.call-update) | async-done | bytes 1048592 | tf_op jit(solution)/shard_map/all_gather | solution.py:68
  105.3 15.5 %while.36 = (s32[]{:T(128)}, f32[1280,128]{1,0:T(8,128)S(1)}, bf16[8,512,128]{2,1,0:T(8,128)(2,1)}, bf16[1280,128]{1,0:T(8,128)(2,1)S(1)}, f32[1280]{0:T(1024)S(1)}, /*index=5*/bf16[8,512,128]{2,1,0:T(8,128)(2,1)}, s32[]{:T(128)}) while((s32[]{:T(128)}, f32[1280,128]{1,0:T(8,128)S(1)}, bf16[8,512,128]{2,1,0:T(8,128)(2,1)}, ...), condition=%wide.region_7.8_spmd, body=%wide.region_6.7_spmd.sunk | while | flops 337674240 | bytes 1906773 | solution.py:125
  105.3 1.9 convolution_add_fusion.5
  107.2 1.9 convolution_add_fusion.5
  109.2 1.9 convolution_add_fusion.5
  111.1 1.9 convolution_add_fusion.5
  113.0 1.9 convolution_add_fusion.5
  115.0 1.9 convolution_add_fusion.5
  116.9 1.9 convolution_add_fusion.5
  118.8 1.9 convolution_add_fusion.5
  120.8 23.3 %all-gather.8.cloned.1.call-done = bf16[1,256,5120]{2,1,0:T(8,128)(2,1)} async-done(((bf16[1,32,5120]{2,1,0:T(8,128)(2,1)}), bf16[1,256,5120]{2,1,0:T(8,128)(2,1)}) %all-gather.8.cloned.1.call-update) | async-done | bytes 2621456 | tf_op jit(solution)/shard_map/all_gather | solution.py:62
  144.1 5.9 %fusion.41 = bf16[256,5,128]{2,0,1:T(8,128)(2,1)S(1)} fusion(bf16[1,5,128,5120]{3,2,1,0:T(8,128)(2,1)} %param.15, bf16[1,256,5120]{2,1,0:T(8,128)(2,1)} %all-gather.8.cloned.1.call-done), kind=kOutput, calls=%fused_computation.54 | convolution fusion | flops 1677885440 | bytes 9502720 | tf_op jit(solution)/shard_map/rsc,ghdc->rsghd/dot_general | solution.py:60
  150.0 1.0 copy.60
  151.0 1.2 reshape_squeeze.12
  152.5 51.2 %while.37 = (s32[]{:T(128)}, f32[1280,128]{1,0:T(8,128)S(1)}, bf16[8,512,2,128]{3,1,2,0:T(8,128)(2,1)}, bf16[8,512,128]{2,1,0:T(8,128)(2,1)}, bf16[1280,128]{1,0...) while((s32[]{:T(128)}, f32[1280,128]{1,0:T(8,128)S(1)}, ...), condition=%wide.region_10.11_spmd.clone, body=%wide.region_9.10_spmd.clone.sunk | while | flops 844955648 | bytes 11675791 | solution.py:157
  152.5 1.5 fusion.126
  154.5 1.5 fusion.127
  156.5 1.7 convolution_add_fusion.6
  158.9 1.5 fusion.126
  160.9 1.5 fusion.127
  162.9 1.7 convolution_add_fusion.6
  165.3 1.5 fusion.126
  167.3 1.5 fusion.127
  169.3 1.7 convolution_add_fusion.6
  171.7 1.5 fusion.126
  173.7 1.5 fusion.127
  175.7 1.7 convolution_add_fusion.6
  178.1 1.5 fusion.126
  180.1 1.5 fusion.127
  182.1 1.7 convolution_add_fusion.6
  184.5 1.5 fusion.126
  186.5 1.5 fusion.127
  188.5 1.7 convolution_add_fusion.6
  190.9 1.5 fusion.126
  192.9 1.5 fusion.127
  194.9 1.7 convolution_add_fusion.6
  197.3 1.5 fusion.126
  199.3 1.5 fusion.127
  201.3 1.7 convolution_add_fusion.6
  203.7 3.1 %copy.68 = bf16[8,512,2,128]{3,1,0,2:T(8,128)(2,1)} copy(bf16[8,512,2,128]{3,1,2,0:T(8,128)(2,1)} %get-tuple-element.117) | data formatting | bytes 4194304 | tf_op jit(solution)/shard_map/convert_element_type | solution.py:166
  209.6 1.1 copy.65
  210.7 1.6 fusion.40
  212.4 0.9 copy.69
  213.3 1.0 fusion.47
  214.3 64.9 %reduce-scatter.2.cloned.1.call-done = bf16[256,1,2,128]{3,0,2,1:T(8,128)(2,1)} async-done(((bf16[4096,1,2,128]{3,0,2,1:T(8,128)(2,1)}), bf16[256,1,2,128]{3,0,2,1:T(8,128)(2,1)}) %reduce-scatter.2.cloned.1.call-update) | async-done | bytes 131088 | tf_op jit(solution)/shard_map/reduce_scatter | solution.py:165
  279.2 1.5 slice_bitcast_fusion
  (121 shorter events, 26.5 us)
Async XLA Ops:
  7.2 69.2 %copy-start = (bf16[1,256,1,128]{3,1,2,0:T(8,128)(2,1)S(1)}, bf16[1,256,1,128]{3,1,2,0:T(8,128)(2,1)}, u32[]{:S(2)}) copy-start(bf16[1,256,1,128]{3,1,2,0:T(8,128)(2,1)} %param.18) | copy-start | bytes 196612
  7.2 52.0 %all-gather.4.cloned.1.call-start = ((), (), s32[]{:S(2)}) async-start(), calls=%async_computation.1 | async-start | bytes 1114112 | tf_op jit(solution)/shard_map/all_gather | solution.py:67
  7.9 97.4 %all-gather.6.cloned.1.call-start = ((), (), s32[]{:S(2)}) async-start(), calls=%async_computation.2 | async-start | bytes 1114112 | tf_op jit(solution)/shard_map/all_gather | solution.py:68
  8.7 135.4 %all-gather.8.cloned.1.call-start = ((), (), s32[]{:S(2)}) async-start(), calls=%async_computation.3 | async-start | bytes 2949120 | tf_op jit(solution)/shard_map/all_gather | solution.py:62
  9.4 269.8 %reduce-scatter.2.cloned.1.call-start = ((), (), s32[]{:S(2)}) async-start(), calls=%async_computation.4 | async-start | bytes 2228224 | tf_op jit(solution)/shard_map/reduce_scatter | solution.py:165
  14.7 3.0 %copy-start.1 = (bf16[1,256,1,5,64]{4,1,3,2,0:T(8,128)(2,1)}, bf16[1,256,1,5,64]{4,1,3,2,0:T(8,128)(2,1)S(1)}, u32[]{:S(2)}) copy-start(bf16[1,256,1,5,64]{4,1,3,2,0:T(8,128)(2,1)S(1)} %get-tuple-element.210) | copy-start | bytes 491524
  14.7 3.0 %copy-start.3 = (bf16[1,256,1,5,64]{4,1,3,2,0:T(8,128)(2,1)}, bf16[1,256,1,5,64]{4,1,3,2,0:T(8,128)(2,1)S(1)}, u32[]{:S(2)}) copy-start(bf16[1,256,1,5,64]{4,1,3,2,0:T(8,128)(2,1)S(1)} %get-tuple-element.211) | copy-start | bytes 491524
  14.7 2.4 copy-start.9
  17.1 1.8 copy-start.7
  17.7 1.2 copy-start.8
  150.0 57.2 %copy-start.5 = (bf16[256,5,128]{2,0,1:T(8,128)(2,1)}, bf16[256,5,128]{2,0,1:T(8,128)(2,1)S(1)}, u32[]{:S(2)}) copy-start(bf16[256,5,128]{2,0,1:T(8,128)(2,1)S(1)} %fusion.41) | copy-start | bytes 983044
  206.8 1.0 copy-start.2
  206.8 1.1 copy-start.4
  208.4 2.3 copy-start.10
  209.6 2.7 copy-start.11
  210.7 2.6 copy-start.6
Sparse Core Ops, SparseCore 0:
  10.5 48.6 all-gather.3
  61.6 43.6 all-gather.5
  106.9 37.1 all-gather.7
  207.0 72.2 reduce-scatter.1
where the time goes:
time: 289 us; the launch traced here: 287 us
  waiting for transfers between devices  158 us (55%)
  matrix products  83.1 us (29%)
  local copies, waits for them, and re-layouts  15.5 us (5%)
  other arithmetic  15.2 us (5%)
  between operations  14.7 us (5%)
    reduce_scatter x1, waiting for transfers between devices, local(): lax.psum_scatter(jnp.stack(term_list, axis=1).astype(jnp.bfloat16), 'roll...  64.9 us
    all_gather x1, waiting for transfers between devices, local(): lax.all_gather(keys_prompt, 'roll', axis=0, tiled=True)  40.1 us
    dot_general x24, matrix products, inner_dot(): lax.dot_general(left, right, (((1,), (1,)), ((), ())), preferred_element_...  34.9 us
    all_gather x1, waiting for transfers between devices, local(): lax.all_gather(values_prompt, 'roll', axis=0, tiled=True)  27.6 us
    all_gather x1, waiting for transfers between devices, local(): lax.all_gather(out_grad, 'kvh', axis=1, tiled=True)  23.3 us
    dot_general x8, matrix products, output_step(): jnp.dot(attn_probs, blocks[1], preferred_element_type=jnp.float32)  15.3 us
    dot_general x8, matrix products, grad_step(): jnp.dot(score_grad, blocks[0], preferred_element_type=jnp.float32)  13.5 us
    dot_general x16, matrix products, outer_sum(): lax.dot_general(left, right, (((0,), (0,)), ((), ())), preferred_element_...  8.11 us
  transfers between devices with their start and end apart: 4, of which 4 were waited for; matrix products, arithmetic and copies ran while one was open for 17% of the time, Pallas kernels for 0%

commit v1 on v0

v1 whole, which is shorter than its diff:
```python
import functools
import math

import jax
import jax.numpy as jnp
import numpy as np
from jax import lax
from jax.experimental import pallas as pl
from jax.experimental.pallas import tpu as pltpu
from jax.sharding import PartitionSpec as P

MESH = pl.DeviceIdType.MESH
f32 = jnp.float32
bf16 = jnp.bfloat16

HEADS = 5
SEQ = 256
HD = 128
ROWS = HEADS * SEQ
HALF = ROWS // 2
BLK = 256
WIDTH = 5120
PROMPT = 4096
CHUNK = 32
SCALE = HD ** -0.5
SCALE2 = SCALE * math.log2(math.e)
PAIRS = 8


def dot(a, b):
    return lax.dot_general(a, b, (((1,), (0,)), ((), ())), preferred_element_type=f32)


def dot_nt(a, b):
    return lax.dot_general(a, b, (((1,), (1,)), ((), ())), preferred_element_type=f32)


def kernel(
    og_hbm, w_hbm, q_hbm, kn_hbm, vn_hbm, kp_hbm, vp_hbm, off_ref, freq_ref,
    dq_ref, dkn_ref, dvn_ref, dkp_ref, dvp_ref,
    w_v, do_v, kb, vb, q_v, kn_v, qt, qp, dot_t, dop, s_v, p_v, o_t, dq_t, m_v, l_v, delta_v,
    cos_v, sin_v, ds_v, ag_v, csend, crecv, zs, zr,
    lsem, ksend, vsend, kfw, vfw, krecv, vrecv, dsend, drecv, cs_sem, cr_sem, zs_sem, zr_sem,
):
    roll = lax.axis_index("roll")
    kvh = lax.axis_index("kvh")
    zz, yh, cc = roll // 4, (roll // 2) % 2, roll % 2
    yl, xx = kvh // 4, kvh % 4

    def dev(dz=0, dyh=0, dc=0, dyl=0, dx=0):
        r = (((zz + dz) % 4) * 2 + (yh + dyh) % 2) * 2 + (cc + dc) % 2
        k = ((yl + dyl) % 2) * 4 + (xx + dx) % 4
        return (r, k)

    core, yhp = dev(dc=1), dev(dyh=1)
    zp, zm, z2 = dev(dz=1), dev(dz=3), dev(dz=2)
    ylp, xp, xm = dev(dyl=1), dev(dx=1), dev(dx=3)

    barrier = pltpu.get_barrier_semaphore()
    for d in (core, yhp, zp, zm, z2, ylp, xp, xm):
        pl.semaphore_signal(barrier, 1, device_id=d, device_id_type=MESH)

    local = [
        pltpu.make_async_copy(kp_hbm, kb.at[15], lsem.at[0]),
        pltpu.make_async_copy(vp_hbm, vb.at[15], lsem.at[1]),
        pltpu.make_async_copy(q_hbm, q_v, lsem.at[2]),
        pltpu.make_async_copy(kn_hbm, kn_v, lsem.at[3]),
        pltpu.make_async_copy(vn_hbm, vb.at[16], lsem.at[4]),
        pltpu.make_async_copy(og_hbm, do_v.at[pl.ds(0, CHUNK)], lsem.at[5]),
        pltpu.make_async_copy(w_hbm, w_v, lsem.at[6]),
    ]
    for c in local:
        c.start()

    pl.semaphore_wait(barrier, 8)

    def remote(src, dst, ssem, rsem, d):
        return pltpu.make_async_remote_copy(
            src_ref=src, dst_ref=dst, send_sem=ssem, recv_sem=rsem, device_id=d, device_id_type=MESH
        )

    first_hops = ((13, yhp), (11, zp), (9, zm), (3, z2), (14, core))
    relay_hops = ((7, zp), (5, zm), (1, z2))

    def kv_own(src, buf, ssem, rsem):
        return [remote(src, buf.at[s], ssem.at[i], rsem.at[s], d) for i, (s, d) in enumerate(first_hops)]

    def kv_relay(buf, ssem, rsem):
        return [
            remote(buf.at[13], buf.at[s], ssem.at[5 + i], rsem.at[s], d) for i, (s, d) in enumerate(relay_hops)
        ]

    def kv_forward(buf, fsem, rsem, n):
        return remote(buf.at[2 * n + 1], buf.at[2 * n], fsem.at[n], rsem.at[2 * n], core)

    def kv_arrived(buf, rsem, ssem, s):
        remote(buf.at[s], buf.at[s], ssem.at[0], rsem.at[s], core).wait_recv()

    for c in kv_own(kp_hbm, kb, ksend, krecv):
        c.start()
    for c in kv_own(vp_hbm, vb, vsend, vrecv):
        c.start()

    def rows(slot, lo=0, size=CHUNK):
        return do_v.at[pl.ds(slot * CHUNK + lo, size)]

    do_own = [
        remote(og_hbm, rows(1), dsend.at[0], drecv.at[0], ylp),
        remote(og_hbm, rows(3), dsend.at[1], drecv.at[1], xp),
        remote(og_hbm, rows(2), dsend.at[2], drecv.at[2], xm),
    ]
    do_relay = [
        remote(rows(3, 0, 16), rows(4, 0, 16), dsend.at[3], drecv.at[3], xp),
        remote(rows(2, 16, 16), rows(4, 16, 16), dsend.at[4], drecv.at[4], xm),
        remote(rows(1), rows(6), dsend.at[5], drecv.at[5], xp),
        remote(rows(1), rows(5), dsend.at[6], drecv.at[6], xm),
        remote(rows(4, 0, 16), rows(7, 0, 16), dsend.at[7], drecv.at[7], ylp),
        remote(rows(4, 16, 16), rows(7, 16, 16), dsend.at[8], drecv.at[8], ylp),
    ]
    for c in do_own:
        c.start()

    def kof(dyl, dx):
        return ((yl + dyl) % 2) * 4 + (xx + dx) % 4

    chunks = [kof(0, 0), kof(1, 0), kof(0, 1), kof(0, 3), kof(0, 2), kof(1, 1), kof(1, 3), kof(1, 2)]

    pos = (off_ref[0] + PROMPT + lax.broadcasted_iota(jnp.int32, (SEQ, HD), 0)).astype(f32)
    angle = pos * freq_ref[...]
    cos_v[...] = jnp.cos(angle)
    lane = lax.broadcasted_iota(jnp.int32, (SEQ, HD), 1)
    sin_a = jnp.sin(angle)
    sin_v[...] = jnp.where(lane < HD // 2, -sin_a, sin_a)

    for i in (2, 3, 4):
        local[i].wait()
    kn = kn_v[...].astype(f32)
    kb[16] = (kn * cos_v[...] + pltpu.roll(kn, HD // 2, 1) * sin_v[...]).astype(bf16)
    for p in range(2):
        for h in range(HEADS):
            parts = []
            for j in range(4):
                k = chunks[4 * p + j]
                x = q_v[pl.ds(pl.multiple_of(h * SEQ + k * CHUNK, CHUNK), CHUNK), :].astype(f32)
                at = pl.ds(pl.multiple_of(k * CHUNK, CHUNK), CHUNK)
                parts.append((x * cos_v[at, :] + pltpu.roll(x, HD // 2, 1) * sin_v[at, :]))
            tile = jnp.concatenate(parts, axis=0)
            qt[:, pl.ds((p * HEADS + h) * HD, HD)] = tile.T.astype(bf16)

    tl = lax.broadcasted_iota(jnp.int32, (1, HD), 1)

    def tokens(p):
        which = tl // CHUNK
        base = jnp.where(
            which == 0,
            chunks[4 * p],
            jnp.where(which == 1, chunks[4 * p + 1], jnp.where(which == 2, chunks[4 * p + 2], chunks[4 * p + 3])),
        )
        return base * CHUNK + tl % CHUNK

    key_at = lax.broadcasted_iota(jnp.int32, (BLK, HD), 0)
    for p in range(2):
        allowed = key_at <= tokens(p)
        for h in range(HEADS):
            at = pl.ds((p * HEADS + h) * HD, HD)
            s = jnp.where(allowed, dot(kb[16], qt[:, at]), -1e30)
            s_v[16, :, at] = s
            m_v[:, at] = jnp.max(s, axis=0, keepdims=True)

    local[0].wait()

    def scores_of(slot):
        kblk = kb[slot]
        for c in range(ROWS // 256):
            at = pl.ds(c * 256, 256)
            s = dot(kblk, qt[:, at])
            s_v[slot, :, at] = s
            m_v[:, at] = jnp.maximum(m_v[:, at], jnp.max(s, axis=0, keepdims=True))

    def score_step(i, carry):
        n = PAIRS - 1 - i

        @pl.when(n < PAIRS - 1)
        def _():
            kv_arrived(kb, krecv, ksend, 2 * n + 1)
            kv_forward(kb, kfw, krecv, n).start()

        @pl.when(n == PAIRS - 2)
        def _():
            for c in kv_relay(kb, ksend, krecv):
                c.start()

        scores_of(2 * n + 1)
        kv_arrived(kb, krecv, ksend, 2 * n)
        scores_of(2 * n)
        return carry

    lax.fori_loop(0, PAIRS, score_step, 0)

    do_own[1].wait_recv()
    do_relay[0].start()
    do_own[2].wait_recv()
    do_relay[1].start()
    do_own[0].wait_recv()
    do_relay[2].start()
    do_relay[3].start()

    def output_of(slot, first=False):
        vt = vb[slot].astype(f32).T.astype(bf16)
        for c in range(ROWS // 256):
            at = pl.ds(c * 256, 256)
            e = jnp.exp2(s_v[slot, :, at] * SCALE2 - m_v[:, at] * SCALE2)
            total = jnp.sum(e, axis=0, keepdims=True)
            eb = e.astype(bf16)
            p_v[slot, :, at] = eb
            o = dot(vt, eb)
            if first:
                l_v[:, at] = total
                o_t[:, at] = o
            else:
                l_v[:, at] += total
                o_t[:, at] += o

    output_of(16, True)
    local[1].wait()

    def output_step(i, carry):
        n = PAIRS - 1 - i

        @pl.when(n < PAIRS - 1)
        def _():
            kv_arrived(vb, vrecv, vsend, 2 * n + 1)
            kv_forward(vb, vfw, vrecv, n).start()

        @pl.when(n == PAIRS - 2)
        def _():
            for c in kv_relay(vb, vsend, vrecv):
                c.start()

        @pl.when(n == 1)
        def _():
            do_relay[0].wait_recv()
            do_relay[4].start()
            do_relay[1].wait_recv()
            do_relay[5].start()

        output_of(2 * n + 1)
        kv_arrived(vb, vrecv, vsend, 2 * n)
        output_of(2 * n)
        return carry

    lax.fori_loop(0, PAIRS, output_step, 0)

    for t in range(ROWS // HD):
        at = pl.ds(t * HD, HD)
        inv = 1.0 / l_v[:, at]
        l_v[:, at] = inv
        o_t[:, at] *= inv
        qp[at, :] = (qt[:, at].astype(f32) * (inv * SCALE)).T.astype(bf16)

    dq_t[...] = jnp.zeros_like(dq_t)

    def start_part(p):
        ag_v[...] = jnp.zeros_like(ag_v)

        def ag_step(i, carry):
            at = pl.ds(pl.multiple_of(i * 1024, 1024), 1024)
            ag_v[...] += dot_nt(w_v[:, at], do_v[p * HD:(p + 1) * HD, at])
            return carry

        lax.fori_loop(0, WIDTH // 1024, ag_step, 0)
        for h in range(HEADS):
            at = pl.ds((p * HEADS + h) * HD, HD)
            g = ag_v[h * HD:(h + 1) * HD, :].astype(bf16)
            dot_t[:, at] = g
            gf = g.astype(f32)
            delta_v[:, at] = jnp.sum(gf * o_t[:, at], axis=0, keepdims=True)
            dop[at, :] = (gf * l_v[:, at]).T.astype(bf16)

    def grads_of(p, slot):
        vblk = vb[slot]
        for c, size in ((0, 256), (256, 256), (512, 128)):
            at = pl.ds(p * HALF + c, size)
            dp = dot(vblk, dot_t[:, at])
            ds_v[:, c:c + size] = (p_v[slot, :, at].astype(f32) * (dp - delta_v[:, at])).astype(bf16)
        part = pl.ds(p * HALF, HALF)
        kt = kb[slot].astype(f32).T.astype(bf16)
        dq_t[:, part] += dot(kt, ds_v[...])
        dk = dot(ds_v[...], qp[part, :])
        dv = dot(p_v[slot, :, part], dop[part, :])
        return dk, dv

    local[5].wait()
    local[6].wait()
    start_part(0)

    def part_a(i, carry):
        dk, dv = grads_of(0, i)
        s_v[i, :, 0:HD] = dk
        s_v[i, :, HD:2 * HD] = dv
        return carry

    lax.fori_loop(0, 17, part_a, 0)

    for i in (2, 3, 4, 5):
        do_relay[i].wait_recv()
    start_part(1)

    def core_copy(n):
        return remote(csend.at[n], crecv.at[n], cs_sem.at[n], cr_sem.at[n], core)

    z_dest = (zm, zp, zp, zm, zp, zm, yhp)

    def z_copy(j):
        return remote(zs.at[j], zr.at[j], zs_sem.at[j], zr_sem.at[j], z_dest[j])

    def part_b(n, carry):
        dk, dv = grads_of(1, 2 * n)
        csend[n, :, 0:HD] = (dk + s_v[2 * n, :, 0:HD]).astype(bf16)
        csend[n, :, HD:2 * HD] = (dv + s_v[2 * n, :, HD:2 * HD]).astype(bf16)
        core_copy(n).start()
        dk, dv = grads_of(1, 2 * n + 1)
        s_v[2 * n + 1, :, 0:HD] += dk
        s_v[2 * n + 1, :, HD:2 * HD] += dv
        core_copy(n).wait_recv()
        total = s_v[2 * n + 1, :, 0:2 * HD] + crecv[n].astype(f32)
        s_v[2 * n + 1, :, 0:2 * HD] = total

        for j, extras in ((3, (0,)), (4, (1,)), (6, (2, 3))):
            @pl.when(n == j)
            def _():
                for e in extras:
                    z_copy(e).wait_recv()
                    s_v[2 * n + 1, :, 0:2 * HD] += zr[e].astype(f32)

        for j in range(7):
            @pl.when(n == j)
            def _():
                zs[j] = s_v[2 * n + 1, :, 0:2 * HD].astype(bf16)
                z_copy(j).start()
        return carry

    lax.fori_loop(0, PAIRS, part_b, 0)

    dk, dv = grads_of(1, 16)
    dk = dk + s_v[16, :, 0:HD]
    dvn_ref[...] = (dv + s_v[16, :, HD:2 * HD]).astype(bf16)
    dkn_ref[...] = (dk * cos_v[...] - pltpu.roll(dk, HD // 2, 1) * sin_v[...]).astype(bf16)

    for p in range(2):
        for h in range(HEADS):
            at = pl.ds((p * HEADS + h) * HD, HD)
            g = (dq_t[:, at] * (l_v[:, at] * SCALE)).T
            for j in range(4):
                k = chunks[4 * p + j]
                x = g[j * CHUNK:(j + 1) * CHUNK, :]
                ta = pl.ds(pl.multiple_of(k * CHUNK, CHUNK), CHUNK)
                y = x * cos_v[ta, :] - pltpu.roll(x, HD // 2, 1) * sin_v[ta, :]
                dq_ref[pl.ds(pl.multiple_of(h * SEQ + k * CHUNK, CHUNK), CHUNK), :] = y.astype(bf16)

    total = s_v[15, :, 0:2 * HD]
    for e in (4, 5, 6):
        z_copy(e).wait_recv()
        total = total + zr[e].astype(f32)
    dkp_ref[...] = total[:, 0:HD].astype(bf16)
    dvp_ref[...] = total[:, HD:2 * HD].astype(bf16)

    for src, buf, ssem, fsem, rsem in ((kp_hbm, kb, ksend, kfw, krecv), (vp_hbm, vb, vsend, vfw, vrecv)):
        for c in kv_own(src, buf, ssem, rsem) + kv_relay(buf, ssem, rsem):
            c.wait_send()
        for n in range(PAIRS - 1):
            kv_forward(buf, fsem, rsem, n).wait_send()
    for c in do_own + do_relay:
        c.wait_send()
    for n in range(PAIRS):
        core_copy(n).wait_send()
    for j in range(7):
        z_copy(j).wait_send()


def local(out_grad, out_weight, queries, keys_new, values_new, keys_prompt, values_prompt, offsets):
    half = HD // 2
    frequency = np.power(np.float32(1000000.0), -(np.arange(half, dtype=np.float32) / half)).astype(np.float32)
    frequency = jnp.asarray(np.concatenate([frequency, frequency])[None, :])
    q = jnp.transpose(queries[0, :, 0], (1, 0, 2)).reshape(ROWS, HD)
    any_spec = pl.BlockSpec(memory_space=pl.ANY)
    vmem = pl.BlockSpec(memory_space=pltpu.VMEM)
    dma = pltpu.SemaphoreType.DMA
    dq, dkn, dvn, dkp, dvp = pl.pallas_call(
        kernel,
        out_shape=(
            jax.ShapeDtypeStruct((ROWS, HD), bf16),
            jax.ShapeDtypeStruct((SEQ, HD), bf16),
            jax.ShapeDtypeStruct((SEQ, HD), bf16),
            jax.ShapeDtypeStruct((BLK, HD), bf16),
            jax.ShapeDtypeStruct((BLK, HD), bf16),
        ),
        in_specs=[any_spec] * 7 + [pl.BlockSpec(memory_space=pltpu.SMEM), vmem],
        out_specs=(vmem,) * 5,
        scratch_shapes=[
            pltpu.VMEM((HEADS * HD, WIDTH), bf16),
            pltpu.VMEM((SEQ, WIDTH), bf16),
            pltpu.VMEM((17, BLK, HD), bf16),
            pltpu.VMEM((17, BLK, HD), bf16),
            pltpu.VMEM((ROWS, HD), bf16),
            pltpu.VMEM((SEQ, HD), bf16),
            pltpu.VMEM((HD, ROWS), bf16),
            pltpu.VMEM((ROWS, HD), bf16),
            pltpu.VMEM((HD, ROWS), bf16),
            pltpu.VMEM((ROWS, HD), bf16),
            pltpu.VMEM((17, BLK, ROWS), f32),
            pltpu.VMEM((17, BLK, ROWS), bf16),
            pltpu.VMEM((HD, ROWS), f32),
            pltpu.VMEM((HD, ROWS), f32),
            pltpu.VMEM((1, ROWS), f32),
            pltpu.VMEM((1, ROWS), f32),
            pltpu.VMEM((1, ROWS), f32),
            pltpu.VMEM((SEQ, HD), f32),
            pltpu.VMEM((SEQ, HD), f32),
            pltpu.VMEM((BLK, HALF), bf16),
            pltpu.VMEM((HEADS * HD, HD), f32),
            pltpu.VMEM((PAIRS, BLK, 2 * HD), bf16),
            pltpu.VMEM((PAIRS, BLK, 2 * HD), bf16),
            pltpu.VMEM((7, BLK, 2 * HD), bf16),
            pltpu.VMEM((7, BLK, 2 * HD), bf16),
            dma((7,)),
            dma((8,)),
            dma((8,)),
            dma((7,)),
            dma((7,)),
            dma((16,)),
            dma((16,)),
            dma((9,)),
            dma((9,)),
            dma((8,)),
            dma((8,)),
            dma((7,)),
            dma((7,)),
        ],
        compiler_params=pltpu.CompilerParams(
            collective_id=0, has_side_effects=True, vmem_limit_bytes=60 * 1024 * 1024
        ),
        name="attention_backward",
    )(
        out_grad[0],
        out_weight.reshape(HEADS * HD, WIDTH),
        q,
        keys_new[0, :, 0],
        values_new[0, :, 0],
        keys_prompt[:, 0],
        values_prompt[:, 0],
        offsets,
        frequency,
    )
    grad_queries = jnp.transpose(dq.reshape(HEADS, SEQ, HD), (1, 0, 2))[None, :, None]
    return (
        grad_queries,
        dkn[None, :, None],
        dvn[None, :, None],
        dkp[:, None],
        dvp[:, None],
    )


def solution(mesh):
    placed = (
        P("roll", "kvh", None),
        P("kvh", None, None, None),
        P("roll", None, "kvh", None, None),
        P("roll", None, "kvh", None),
        P("roll", None, "kvh", None),
        P("roll", "kvh", None),
        P("roll", "kvh", None),
        P("roll"),
    )
    return jax.shard_map(
        local,
        mesh=mesh,
        in_specs=placed,
        out_specs=(
            P("roll", None, "kvh", None, None),
            P("roll", None, "kvh", None),
            P("roll", None, "kvh", None),
            P("roll", "kvh", None),
            P("roll", "kvh", None),
        ),
        check_vma=False,
    )
```

time: 289 us -> 79.6 us (0.28)
  waiting for transfers between devices: 158 us -> 0 us
  matrix products: 83.1 us -> 0 us
  Pallas kernels: 0 us -> 70.3 us
  other arithmetic: 15.2 us -> 0 us
  between operations: 14.7 us -> 1.29 us
  local copies, waits for them, and re-layouts: 15.5 us -> 7.61 us
    all_gather x3 -> x0, waiting for transfers between devices: 91 us -> none  [the longest x1 40.1 us: local(): lax.all_gather(keys_prompt, 'roll', axis=0, tiled=True)]
    dot_general x63 -> x0, matrix products: 83.1 us -> none  [the longest x24 34.9 us: inner_dot(): lax.dot_general(left, right, (((1,), (1,)), ((), ())), preferred_element_...]
    pallas_call x0 -> x1, Pallas kernels: none -> 70.3 us  [local(): pl.pallas_call(kernel, out_shape=(jax.ShapeDtypeStruct((ROWS, HD), bf16),...]
    reduce_scatter x1 -> x0, waiting for transfers between devices: 64.9 us -> none  [local(): lax.psum_scatter(jnp.stack(term_list, axis=1).astype(jnp.bfloat16), 'roll...]
    convert_element_type x4 -> x0, local copies, waits for them, and re-layouts: 6.1 us -> none  [the longest x1 3.13 us: local(): jnp.stack(term_list, axis=1).astype(jnp.bfloat16)]
    dynamic_update_slice x8 -> x0, other arithmetic: 5.8 us -> none  [local(): lax.scan(grad_step, zero_rows, (key_blocks, value_blocks))]
    unnamed x26 -> x5, local copies, waits for them, and re-layouts: 2.06 us -> 7.61 us
    reduce_sum x10 -> x0, other arithmetic: 3.95 us -> none  [the longest x8 3.25 us: stat_step(): jnp.sum(jnp.exp(scores - new_max[:, None]), axis=1)]
  transfers between devices with their start and end apart: 4 -> 0, of which waited for: 4 -> 0; matrix products, arithmetic and copies ran while one was open for 17% -> 0% of each run, Pallas kernels for 0% -> 0%
where the time goes in v1:
time: 79.6 us; the launch traced here: 79.2 us
  Pallas kernels  70.3 us (88%)
  local copies, waits for them, and re-layouts  7.61 us (10%)
  between operations  1.29 us (2%)
    pallas_call x1, Pallas kernels, local(): pl.pallas_call(kernel, out_shape=(jax.ShapeDtypeStruct((ROWS, HD), bf16),...  70.3 us
    unnamed x5, local copies, waits for them, and re-layouts  7.61 us

profile of v1, /device:TPU:1, one launch (start us, length us, event | category | flops | bytes accessed | tf_op | source)
XLA Modules:
  0.0 79.2 jit_solution(13870832912430008195)
XLA Ops:
  1.3 70.3 %attention_backward.1 = (bf16[1280,128]{1,0:T(8,128)(2,1)}, bf16[256,128]{1,0:T(8,128)(2,1)}, bf16[256,128]{1,0:T(8,128)(2,1)}, bf16[256,128]{1,0:T(8,128)(2,1)}, bf16[256,128]{1,0:T(8,128)(2,1)}) custom-call(bf16[32,5120]{1,0:T(8,128)(2,1)} %bitcast.21, bf16[640,5120]{1,0:T(8,128)(2,1)} %bitcast.20, bf16[1280,128]{1,0:T(8,128)(2,1)} %bitcast.22, ...), custom_call_target="tpu_custom_call" | custom-call | tf_op jit(solution)/shard_map/attention_backward/pallas_call | solution.py:389
  71.6 1.7 %copy.20 = bf16[1,256,1,5,128]{4,1,3,2,0:T(8,128)(2,1)} copy(bf16[1,256,1,5,128]{4,1,3,2,0:T(8,128)(2,1)} %bitcast.23) | data formatting | bytes 655360
  73.3 1.5 %copy.21 = bf16[1,256,1,128]{3,1,2,0:T(8,128)(2,1)} copy(bf16[1,256,1,128]{3,1,2,0:T(8,128)(2,1)} %bitcast.31) | data formatting | bytes 131072
  74.8 1.5 %copy.22 = bf16[1,256,1,128]{3,1,2,0:T(8,128)(2,1)} copy(bf16[1,256,1,128]{3,1,2,0:T(8,128)(2,1)} %bitcast.30) | data formatting | bytes 131072
  76.3 1.5 %copy.23 = bf16[256,1,128]{2,0,1:T(8,128)(2,1)} copy(bf16[256,1,128]{2,0,1:T(8,128)(2,1)} %bitcast.29) | data formatting | bytes 131072
  77.7 1.5 %copy.24 = bf16[256,1,128]{2,0,1:T(8,128)(2,1)} copy(bf16[256,1,128]{2,0,1:T(8,128)(2,1)} %bitcast.28) | data formatting | bytes 131072

commit v2 on v1

--- a/solution.py
+++ b/solution.py
@@ -25,6 +25,8 @@
 SCALE = HD ** -0.5
 SCALE2 = SCALE * math.log2(math.e)
 PAIRS = 8
+PAIR = 2 * BLK
+OWN = slice(16 * BLK, 17 * BLK)
 
 
 def dot(a, b):
@@ -38,7 +40,7 @@
 def kernel(
     og_hbm, w_hbm, q_hbm, kn_hbm, vn_hbm, kp_hbm, vp_hbm, off_ref, freq_ref,
     dq_ref, dkn_ref, dvn_ref, dkp_ref, dvp_ref,
-    w_v, do_v, kb, vb, q_v, kn_v, qt, qp, dot_t, dop, s_v, p_v, o_t, dq_t, m_v, l_v, delta_v,
+    w_v, do_v, kb, vb, kt_v, q_v, kn_v, qt, qp, dot_t, dop, s_v, p_v, o_t, dq_t, m_v, l_v, delta_v,
     cos_v, sin_v, ds_v, ag_v, csend, crecv, zs, zr,
     lsem, ksend, vsend, kfw, vfw, krecv, vrecv, dsend, drecv, cs_sem, cr_sem, zs_sem, zr_sem,
 ):
@@ -61,40 +63,50 @@
         pl.semaphore_signal(barrier, 1, device_id=d, device_id_type=MESH)
 
     local = [
-        pltpu.make_async_copy(kp_hbm, kb.at[15], lsem.at[0]),
-        pltpu.make_async_copy(vp_hbm, vb.at[15], lsem.at[1]),
+        pltpu.make_async_copy(kp_hbm, kb.at[pl.ds(15 * BLK, BLK)], lsem.at[0]),
+        pltpu.make_async_copy(vp_hbm, vb.at[pl.ds(15 * BLK, BLK)], lsem.at[1]),
         pltpu.make_async_copy(q_hbm, q_v, lsem.at[2]),
         pltpu.make_async_copy(kn_hbm, kn_v, lsem.at[3]),
-        pltpu.make_async_copy(vn_hbm, vb.at[16], lsem.at[4]),
+        pltpu.make_async_copy(vn_hbm, vb.at[pl.ds(16 * BLK, BLK)], lsem.at[4]),
         pltpu.make_async_copy(og_hbm, do_v.at[pl.ds(0, CHUNK)], lsem.at[5]),
         pltpu.make_async_copy(w_hbm, w_v, lsem.at[6]),
     ]
     for c in local:
         c.start()
 
+    pos = (off_ref[0] + PROMPT + lax.broadcasted_iota(jnp.int32, (SEQ, HD), 0)).astype(f32)
+    angle = pos * freq_ref[...]
+    cos_v[...] = jnp.cos(angle)
+    lane = lax.broadcasted_iota(jnp.int32, (SEQ, HD), 1)
+    sin_a = jnp.sin(angle)
+    sin_v[...] = jnp.where(lane < HD // 2, -sin_a, sin_a)
+
     pl.semaphore_wait(barrier, 8)
+
+    def blk(buf, slot):
+        return buf.at[pl.ds(slot * BLK, BLK)]
 
     def remote(src, dst, ssem, rsem, d):
         return pltpu.make_async_remote_copy(
             src_ref=src, dst_ref=dst, send_sem=ssem, recv_sem=rsem, device_id=d, device_id_type=MESH
         )
 
-    first_hops = ((13, yhp), (11, zp), (9, zm), (3, z2), (14, core))
-    relay_hops = ((7, zp), (5, zm), (1, z2))
+    first_hops = ((13, yhp), (9, zp), (11, zm), (5, z2), (14, core))
+    relay_hops = ((7, zp), (3, zm), (1, z2))
 
     def kv_own(src, buf, ssem, rsem):
-        return [remote(src, buf.at[s], ssem.at[i], rsem.at[s], d) for i, (s, d) in enumerate(first_hops)]
+        return [remote(src, blk(buf, s), ssem.at[i], rsem.at[s], d) for i, (s, d) in enumerate(first_hops)]
 
     def kv_relay(buf, ssem, rsem):
         return [
-            remote(buf.at[13], buf.at[s], ssem.at[5 + i], rsem.at[s], d) for i, (s, d) in enumerate(relay_hops)
+            remote(blk(buf, 13), blk(buf, s), ssem.at[5 + i], rsem.at[s], d) for i, (s, d) in enumerate(relay_hops)
         ]
 
     def kv_forward(buf, fsem, rsem, n):
-        return remote(buf.at[2 * n + 1], buf.at[2 * n], fsem.at[n], rsem.at[2 * n], core)
+        return remote(blk(buf, 2 * n + 1), blk(buf, 2 * n), fsem.at[n], rsem.at[2 * n], core)
 
     def kv_arrived(buf, rsem, ssem, s):
-        remote(buf.at[s], buf.at[s], ssem.at[0], rsem.at[s], core).wait_recv()
+        remote(blk(buf, s), blk(buf, s), ssem.at[0], rsem.at[s], core).wait_recv()
 
     for c in kv_own(kp_hbm, kb, ksend, krecv):
         c.start()
@@ -125,17 +137,10 @@
 
     chunks = [kof(0, 0), kof(1, 0), kof(0, 1), kof(0, 3), kof(0, 2), kof(1, 1), kof(1, 3), kof(1, 2)]
 
-    pos = (off_ref[0] + PROMPT + lax.broadcasted_iota(jnp.int32, (SEQ, HD), 0)).astype(f32)
-    angle = pos * freq_ref[...]
-    cos_v[...] = jnp.cos(angle)
-    lane = lax.broadcasted_iota(jnp.int32, (SEQ, HD), 1)
-    sin_a = jnp.sin(angle)
-    sin_v[...] = jnp.where(lane < HD // 2, -sin_a, sin_a)
-
     for i in (2, 3, 4):
         local[i].wait()
     kn = kn_v[...].astype(f32)
-    kb[16] = (kn * cos_v[...] + pltpu.roll(kn, HD // 2, 1) * sin_v[...]).astype(bf16)
+    kb[OWN, :] = (kn * cos_v[...] + pltpu.roll(kn, HD // 2, 1) * sin_v[...]).astype(bf16)
     for p in range(2):
         for h in range(HEADS):
             parts = []
@@ -159,60 +164,74 @@
         return base * CHUNK + tl % CHUNK
 
     key_at = lax.broadcasted_iota(jnp.int32, (BLK, HD), 0)
+    kt_v[:, OWN] = kb[OWN, :].T
     for p in range(2):
         allowed = key_at <= tokens(p)
         for h in range(HEADS):
             at = pl.ds((p * HEADS + h) * HD, HD)
-            s = jnp.where(allowed, dot(kb[16], qt[:, at]), -1e30)
-            s_v[16, :, at] = s
+            s = jnp.where(allowed, dot(kb[OWN, :], qt[:, at]), -1e30)
+            s_v[OWN, at] = s
             m_v[:, at] = jnp.max(s, axis=0, keepdims=True)
 
     local[0].wait()
 
-    def scores_of(slot):
-        kblk = kb[slot]
+    def pair_at(n):
+        return pl.multiple_of(n * PAIR, PAIR)
+
+    def scores_of(n):
+        here = pl.ds(pair_at(n), PAIR)
+        kblk = kb[here, :]
+        kt_v[:, here] = kblk.T
         for c in range(ROWS // 256):
             at = pl.ds(c * 256, 256)
             s = dot(kblk, qt[:, at])
-            s_v[slot, :, at] = s
+            s_v[here, at] = s
             m_v[:, at] = jnp.maximum(m_v[:, at], jnp.max(s, axis=0, keepdims=True))
 
+    def gather_order(i):
+        return PAIRS - 1 - i - (i == 4).astype(jnp.int32) + (i == 5).astype(jnp.int32)
+
     def score_step(i, carry):
-        n = PAIRS - 1 - i
-
-        @pl.when(n < PAIRS - 1)
+        n = gather_order(i)
+
+        @pl.when(i > 0)
         def _():
             kv_arrived(kb, krecv, ksend, 2 * n + 1)
             kv_forward(kb, kfw, krecv, n).start()
 
-        @pl.when(n == PAIRS - 2)
+        @pl.when(i == 1)
         def _():
             for c in kv_relay(kb, ksend, krecv):
                 c.start()
-
-        scores_of(2 * n + 1)
+            kv_arrived(vb, vrecv, vsend, 13)
+            for c in kv_relay(vb, vsend, vrecv):
+                c.start()
+
+        @pl.when(i == 5)
+        def _():
+            do_own[1].wait_recv()
+            do_relay[0].start()
+            do_own[2].wait_recv()
+            do_relay[1].start()
+            do_own[0].wait_recv()
+            do_relay[2].start()
+            do_relay[3].start()
+
         kv_arrived(kb, krecv, ksend, 2 * n)
-        scores_of(2 * n)
+        scores_of(n)
         return carry
 
     lax.fori_loop(0, PAIRS, score_step, 0)
 
-    do_own[1].wait_recv()
-    do_relay[0].start()
-    do_own[2].wait_recv()
-    do_relay[1].start()
-    do_own[0].wait_recv()
-    do_relay[2].start()
-    do_relay[3].start()
-
-    def output_of(slot, first=False):
-        vt = vb[slot].astype(f32).T.astype(bf16)
+    def output_of(at_row, size, first=False):
+        here = pl.ds(at_row, size)
+        vt = vb[here, :].T
         for c in range(ROWS // 256):
             at = pl.ds(c * 256, 256)
-            e = jnp.exp2(s_v[slot, :, at] * SCALE2 - m_v[:, at] * SCALE2)
+            e = jnp.exp2(s_v[here, at] * SCALE2 - m_v[:, at] * SCALE2)
             total = jnp.sum(e, axis=0, keepdims=True)
             eb = e.astype(bf16)
-            p_v[slot, :, at] = eb
+            p_v[here, at] = eb
             o = dot(vt, eb)
             if first:
                 l_v[:, at] = total
@@ -221,32 +240,30 @@
                 l_v[:, at] += total
                 o_t[:, at] += o
 
-    output_of(16, True)
+    output_of(16 * BLK, BLK, True)
     local[1].wait()
 
     def output_step(i, carry):
-        n = PAIRS - 1 - i
-
-        @pl.when(n < PAIRS - 1)
+        n = gather_order(i)
+
+        @pl.when(i == 1)
+        def _():
+            kv_forward(vb, vfw, vrecv, n).start()
+
+        @pl.when(i > 1)
         def _():
             kv_arrived(vb, vrecv, vsend, 2 * n + 1)
             kv_forward(vb, vfw, vrecv, n).start()
 
-        @pl.when(n == PAIRS - 2)
-        def _():
-            for c in kv_relay(vb, vsend, vrecv):
-                c.start()
-
-        @pl.when(n == 1)
+        @pl.when(i == 1)
         def _():
             do_relay[0].wait_recv()
             do_relay[4].start()
             do_relay[1].wait_recv()
             do_relay[5].start()
 
-        output_of(2 * n + 1)
         kv_arrived(vb, vrecv, vsend, 2 * n)
-        output_of(2 * n)
+        output_of(pair_at(n), PAIR)
         return carry
 
     lax.fori_loop(0, PAIRS, output_step, 0)
@@ -277,30 +294,34 @@
             delta_v[:, at] = jnp.sum(gf * o_t[:, at], axis=0, keepdims=True)
             dop[at, :] = (gf * l_v[:, at]).T.astype(bf16)
 
-    def grads_of(p, slot):
-        vblk = vb[slot]
-        for c, size in ((0, 256), (256, 256), (512, 128)):
-            at = pl.ds(p * HALF + c, size)
+    def grads_of(p, at_row, size):
+        here = pl.ds(at_row, size)
+        vblk = vb[here, :]
+        for c, width in ((0, 256), (256, 256), (512, 128)):
+            at = pl.ds(p * HALF + c, width)
             dp = dot(vblk, dot_t[:, at])
-            ds_v[:, c:c + size] = (p_v[slot, :, at].astype(f32) * (dp - delta_v[:, at])).astype(bf16)
+            ds_v[0:size, c:c + width] = (p_v[here, at].astype(f32) * (dp - delta_v[:, at])).astype(bf16)
         part = pl.ds(p * HALF, HALF)
-        kt = kb[slot].astype(f32).T.astype(bf16)
-        dq_t[:, part] += dot(kt, ds_v[...])
-        dk = dot(ds_v[...], qp[part, :])
-        dv = dot(p_v[slot, :, part], dop[part, :])
+        dq_t[:, part] += dot(kt_v[:, here], ds_v[0:size, :])
+        dk = dot(ds_v[0:size, :], qp[part, :])
+        dv = dot(p_v[here, part], dop[part, :])
         return dk, dv
 
     local[5].wait()
     local[6].wait()
     start_part(0)
 
-    def part_a(i, carry):
-        dk, dv = grads_of(0, i)
-        s_v[i, :, 0:HD] = dk
-        s_v[i, :, HD:2 * HD] = dv
+    def part_a(n, carry):
+        here = pl.ds(pair_at(n), PAIR)
+        dk, dv = grads_of(0, pair_at(n), PAIR)
+        s_v[here, 0:HD] = dk
+        s_v[here, HD:2 * HD] = dv
         return carry
 
-    lax.fori_loop(0, 17, part_a, 0)
+    lax.fori_loop(0, PAIRS, part_a, 0)
+    dk, dv = grads_of(0, 16 * BLK, BLK)
+    s_v[OWN, 0:HD] = dk
+    s_v[OWN, HD:2 * HD] = dv
 
     for i in (2, 3, 4, 5):
         do_relay[i].wait_recv()
@@ -309,42 +330,49 @@
     def core_copy(n):
         return remote(csend.at[n], crecv.at[n], cs_sem.at[n], cr_sem.at[n], core)
 
-    z_dest = (zm, zp, zp, zm, zp, zm, yhp)
+    z_dest = (zm, zp, zp, zm, zm, zp, yhp)
 
     def z_copy(j):
         return remote(zs.at[j], zr.at[j], zs_sem.at[j], zr_sem.at[j], z_dest[j])
 
+    def own_half(n):
+        return pl.ds(pl.multiple_of(n * PAIR + BLK, BLK), BLK)
+
+    def finish(n, j, extras):
+        total = s_v[own_half(n), 0:2 * HD] + crecv[n].astype(f32)
+        for e in extras:
+            z_copy(e).wait_recv()
+            total = total + zr[e].astype(f32)
+        if j < 7:
+            zs[j] = total.astype(bf16)
+            z_copy(j).start()
+        else:
+            dkp_ref[...] = total[:, 0:HD].astype(bf16)
+            dvp_ref[...] = total[:, HD:2 * HD].astype(bf16)
+
+    extras_of = ((), (), (), (0,), (), (2,), (1, 3), (4, 5, 6))
+
     def part_b(n, carry):
-        dk, dv = grads_of(1, 2 * n)
-        csend[n, :, 0:HD] = (dk + s_v[2 * n, :, 0:HD]).astype(bf16)
-        csend[n, :, HD:2 * HD] = (dv + s_v[2 * n, :, HD:2 * HD]).astype(bf16)
+        dk, dv = grads_of(1, pair_at(n), PAIR)
+        there = pl.ds(pair_at(n), BLK)
+        csend[n, :, 0:HD] = (dk[0:BLK] + s_v[there, 0:HD]).astype(bf16)
+        csend[n, :, HD:2 * HD] = (dv[0:BLK] + s_v[there, HD:2 * HD]).astype(bf16)
         core_copy(n).start()
-        dk, dv = grads_of(1, 2 * n + 1)
-        s_v[2 * n + 1, :, 0:HD] += dk
-        s_v[2 * n + 1, :, HD:2 * HD] += dv
-        core_copy(n).wait_recv()
-        total = s_v[2 * n + 1, :, 0:2 * HD] + crecv[n].astype(f32)
-        s_v[2 * n + 1, :, 0:2 * HD] = total
-
-        for j, extras in ((3, (0,)), (4, (1,)), (6, (2, 3))):
-            @pl.when(n == j)
+        s_v[own_half(n), 0:HD] += dk[BLK:]
+        s_v[own_half(n), HD:2 * HD] += dv[BLK:]
+
+        for j in range(7):
+            @pl.when(n == j + 1)
             def _():
-                for e in extras:
-                    z_copy(e).wait_recv()
-                    s_v[2 * n + 1, :, 0:2 * HD] += zr[e].astype(f32)
-
-        for j in range(7):
-            @pl.when(n == j)
-            def _():
-                zs[j] = s_v[2 * n + 1, :, 0:2 * HD].astype(bf16)
-                z_copy(j).start()
+                core_copy(j).wait_recv()
+                finish(j, j, extras_of[j])
         return carry
 
     lax.fori_loop(0, PAIRS, part_b, 0)
 
-    dk, dv = grads_of(1, 16)
-    dk = dk + s_v[16, :, 0:HD]
-    dvn_ref[...] = (dv + s_v[16, :, HD:2 * HD]).astype(bf16)
+    dk, dv = grads_of(1, 16 * BLK, BLK)
+    dk = dk + s_v[OWN, 0:HD]
+    dvn_ref[...] = (dv + s_v[OWN, HD:2 * HD]).astype(bf16)
     dkn_ref[...] = (dk * cos_v[...] - pltpu.roll(dk, HD // 2, 1) * sin_v[...]).astype(bf16)
 
     for p in range(2):
@@ -358,12 +386,8 @@
                 y = x * cos_v[ta, :] - pltpu.roll(x, HD // 2, 1) * sin_v[ta, :]
                 dq_ref[pl.ds(pl.multiple_of(h * SEQ + k * CHUNK, CHUNK), CHUNK), :] = y.astype(bf16)
 
-    total = s_v[15, :, 0:2 * HD]
-    for e in (4, 5, 6):
-        z_copy(e).wait_recv()
-        total = total + zr[e].astype(f32)
-    dkp_ref[...] = total[:, 0:HD].astype(bf16)
-    dvp_ref[...] = total[:, HD:2 * HD].astype(bf16)
+    core_copy(7).wait_recv()
+    finish(7, 7, extras_of[7])
 
     for src, buf, ssem, fsem, rsem in ((kp_hbm, kb, ksend, kfw, krecv), (vp_hbm, vb, vsend, vfw, vrecv)):
         for c in kv_own(src, buf, ssem, rsem) + kv_relay(buf, ssem, rsem):
@@ -378,6 +402,15 @@
         z_copy(j).wait_send()
 
 
+def hand_over(*refs):
+    sources, results, sems = refs[:5], refs[5:10], refs[10]
+    copies = [pltpu.make_async_copy(a, b, sems.at[i]) for i, (a, b) in enumerate(zip(sources, results))]
+    for c in copies:
+        c.start()
+    for c in copies:
+        c.wait()
+
+
 def local(out_grad, out_weight, queries, keys_new, values_new, keys_prompt, values_prompt, offsets):
     half = HD // 2
     frequency = np.power(np.float32(1000000.0), -(np.arange(half, dtype=np.float32) / half)).astype(np.float32)
@@ -386,7 +419,7 @@
     any_spec = pl.BlockSpec(memory_space=pl.ANY)
     vmem = pl.BlockSpec(memory_space=pltpu.VMEM)
     dma = pltpu.SemaphoreType.DMA
-    dq, dkn, dvn, dkp, dvp = pl.pallas_call(
+    grads = pl.pallas_call(
         kernel,
         out_shape=(
             jax.ShapeDtypeStruct((ROWS, HD), bf16),
@@ -400,16 +433,17 @@
         scratch_shapes=[
             pltpu.VMEM((HEADS * HD, WIDTH), bf16),
             pltpu.VMEM((SEQ, WIDTH), bf16),
-            pltpu.VMEM((17, BLK, HD), bf16),
-            pltpu.VMEM((17, BLK, HD), bf16),
+            pltpu.VMEM((17 * BLK, HD), bf16),
+            pltpu.VMEM((17 * BLK, HD), bf16),
+            pltpu.VMEM((HD, 17 * BLK), bf16),
             pltpu.VMEM((ROWS, HD), bf16),
             pltpu.VMEM((SEQ, HD), bf16),
             pltpu.VMEM((HD, ROWS), bf16),
             pltpu.VMEM((ROWS, HD), bf16),
             pltpu.VMEM((HD, ROWS), bf16),
             pltpu.VMEM((ROWS, HD), bf16),
-            pltpu.VMEM((17, BLK, ROWS), f32),
-            pltpu.VMEM((17, BLK, ROWS), bf16),
+            pltpu.VMEM((17 * BLK, ROWS), f32),
+            pltpu.VMEM((17 * BLK, ROWS), bf16),
             pltpu.VMEM((HD, ROWS), f32),
             pltpu.VMEM((HD, ROWS), f32),
             pltpu.VMEM((1, ROWS), f32),
@@ -417,7 +451,7 @@
             pltpu.VMEM((1, ROWS), f32),
             pltpu.VMEM((SEQ, HD), f32),
             pltpu.VMEM((SEQ, HD), f32),
-            pltpu.VMEM((BLK, HALF), bf16),
+            pltpu.VMEM((PAIR, HALF), bf16),
             pltpu.VMEM((HEADS * HD, HD), f32),
             pltpu.VMEM((PAIRS, BLK, 2 * HD), bf16),
             pltpu.VMEM((PAIRS, BLK, 2 * HD), bf16),
@@ -452,6 +486,14 @@
         offsets,
         frequency,
     )
+    dq, dkn, dvn, dkp, dvp = pl.pallas_call(
+        hand_over,
+        out_shape=tuple(jax.ShapeDtypeStruct(g.shape, g.dtype) for g in grads),
+        in_specs=[any_spec] * 5,
+        out_specs=(any_spec,) * 5,
+        scratch_shapes=[dma((5,))],
+        name="hand_over",
+    )(*grads)
     grad_queries = jnp.transpose(dq.reshape(HEADS, SEQ, HD), (1, 0, 2))[None, :, None]
     return (
         grad_queries,

time: 79.6 us -> 89.5 us (1.12)
  Pallas kernels: 70.3 us -> 88.1 us
  local copies, waits for them, and re-layouts: 7.61 us -> 0 us
    pallas_call x0 -> x1, Pallas kernels: none -> 19 us  [local(): pl.pallas_call(hand_over, out_shape=tuple((jax.ShapeDtypeStruct(g.shape,...]
    unnamed x5 -> x0, local copies, waits for them, and re-layouts: 7.61 us -> none
    pallas_call x1, Pallas kernels: 70.3 us -> 69.1 us  [local(): pl.pallas_call(kernel, out_shape=(jax.ShapeDtypeStruct((ROWS, HD), bf16),...]
where the time goes in v2:
time: 89.5 us; the launch traced here: 89.4 us
  Pallas kernels  88.1 us (98%)
  between operations  1.29 us (1%)
    pallas_call x1, Pallas kernels, local(): pl.pallas_call(kernel, out_shape=(jax.ShapeDtypeStruct((ROWS, HD), bf16),...  69.1 us
    pallas_call x1, Pallas kernels, local(): pl.pallas_call(hand_over, out_shape=tuple((jax.ShapeDtypeStruct(g.shape,...  19 us

profile of v2, /device:TPU:1, one launch (start us, length us, event | category | flops | bytes accessed | tf_op | source)
XLA Modules:
  0.0 89.4 jit_solution(494577657140284454)
XLA Ops:
  1.3 69.1 %attention_backward.1 = (bf16[1280,128]{1,0:T(8,128)(2,1)}, bf16[256,128]{1,0:T(8,128)(2,1)}, bf16[256,128]{1,0:T(8,128)(2,1)}, bf16[256,128]{1,0:T(8,128)(2,1)}, bf16[256,128]{1,0:T(8,128)(2,1)}) custom-call(bf16[32,5120]{1,0:T(8,128)(2,1)} %bitcast.21, bf16[640,5120]{1,0:T(8,128)(2,1)} %bitcast.20, bf16[1280,128]{1,0:T(8,128)(2,1)} %bitcast.22, ...), custom_call_target="tpu_custom_call" | custom-call | tf_op jit(solution)/shard_map/attention_backward/pallas_call | solution.py:422
  70.4 19.0 %hand_over.1 = (bf16[1280,128]{1,0:T(8,128)(2,1)}, bf16[256,128]{1,0:T(8,128)(2,1)}, bf16[256,128]{1,0:T(8,128)(2,1)}, bf16[256,128]{1,0:T(8,128)(2,1)}, bf16[256,128]{1,0:T(8,128)(2,1)}) custom-call(bf16[1280,128]{1,0:T(8,128)(2,1)} %get-tuple-element.15.refs_0_, bf16[256,128]{1,0:T(8,128)(2,1)} %get-tuple-element.16.refs_1_, ...), custom_call_target="tpu_custom_call" | custom-call | tf_op jit(solution)/shard_map/hand_over/pallas_call | solution.py:489

commit v3 on v2

--- a/solution.py
+++ b/solution.py
@@ -17,7 +17,6 @@
 SEQ = 256
 HD = 128
 ROWS = HEADS * SEQ
-HALF = ROWS // 2
 BLK = 256
 WIDTH = 5120
 PROMPT = 4096
@@ -55,11 +54,11 @@
         return (r, k)
 
     core, yhp = dev(dc=1), dev(dyh=1)
-    zp, zm, z2 = dev(dz=1), dev(dz=3), dev(dz=2)
+    zp, zm = dev(dz=1), dev(dz=3)
     ylp, xp, xm = dev(dyl=1), dev(dx=1), dev(dx=3)
 
     barrier = pltpu.get_barrier_semaphore()
-    for d in (core, yhp, zp, zm, z2, ylp, xp, xm):
+    for d in (core, yhp, zp, zm, ylp, xp, xm):
         pl.semaphore_signal(barrier, 1, device_id=d, device_id_type=MESH)
 
     local = [
@@ -81,36 +80,57 @@
     sin_a = jnp.sin(angle)
     sin_v[...] = jnp.where(lane < HD // 2, -sin_a, sin_a)
 
-    pl.semaphore_wait(barrier, 8)
-
-    def blk(buf, slot):
-        return buf.at[pl.ds(slot * BLK, BLK)]
+    pl.semaphore_wait(barrier, 7)
 
     def remote(src, dst, ssem, rsem, d):
         return pltpu.make_async_remote_copy(
             src_ref=src, dst_ref=dst, send_sem=ssem, recv_sem=rsem, device_id=d, device_id_type=MESH
         )
 
-    first_hops = ((13, yhp), (9, zp), (11, zm), (5, z2), (14, core))
-    relay_hops = ((7, zp), (3, zm), (1, z2))
-
-    def kv_own(src, buf, ssem, rsem):
-        return [remote(src, blk(buf, s), ssem.at[i], rsem.at[s], d) for i, (s, d) in enumerate(first_hops)]
-
-    def kv_relay(buf, ssem, rsem):
-        return [
-            remote(blk(buf, 13), blk(buf, s), ssem.at[5 + i], rsem.at[s], d) for i, (s, d) in enumerate(relay_hops)
-        ]
-
-    def kv_forward(buf, fsem, rsem, n):
-        return remote(blk(buf, 2 * n + 1), blk(buf, 2 * n), fsem.at[n], rsem.at[2 * n], core)
-
-    def kv_arrived(buf, rsem, ssem, s):
-        remote(blk(buf, s), blk(buf, s), ssem.at[0], rsem.at[s], core).wait_recv()
-
-    for c in kv_own(kp_hbm, kb, ksend, krecv):
-        c.start()
-    for c in kv_own(vp_hbm, vb, vsend, vrecv):
+    def blk(buf, slot, lo=0, size=BLK):
+        return buf.at[pl.ds(slot * BLK + lo, size)]
+
+    class Spread:
+        def __init__(self, src, buf, send, recv, fsend):
+            self.src, self.buf, self.send, self.recv, self.fsend = src, buf, send, recv, fsend
+            mid = BLK // 2
+            self.near = [self.hop(src, 13, 0, yhp), self.hop(src, 14, 1, core)]
+            self.along = [self.hop(src, 9, 2, zp), self.hop(src, 11, 3, zm)]
+            self.relay = [self.hop(blk(buf, 13), 7, 4, zp), self.hop(blk(buf, 13), 3, 5, zm)]
+            self.far = {
+                9: remote(blk(buf, 9, 0, mid), blk(buf, 5, 0, mid), send.at[6], recv.at[5], zp),
+                11: remote(blk(buf, 11, mid, mid), blk(buf, 5, mid, mid), send.at[7], recv.at[16], zm),
+                7: remote(blk(buf, 7, 0, mid), blk(buf, 1, 0, mid), send.at[8], recv.at[1], zp),
+                3: remote(blk(buf, 3, mid, mid), blk(buf, 1, mid, mid), send.at[9], recv.at[17], zm),
+            }
+
+        def hop(self, src, slot, i, d):
+            return remote(src, blk(self.buf, slot), self.send.at[i], self.recv.at[slot], d)
+
+        def forward(self, n):
+            return remote(
+                blk(self.buf, 2 * n + 1), blk(self.buf, 2 * n), self.fsend.at[n], self.recv.at[2 * n], core
+            )
+
+        def arrived(self, slot):
+            if slot == 5:
+                self.far[9].wait_recv()
+                self.far[11].wait_recv()
+            elif slot == 1:
+                self.far[7].wait_recv()
+                self.far[3].wait_recv()
+            else:
+                self.hop(blk(self.buf, slot), slot, 0, core).wait_recv()
+
+        def wait_send(self):
+            for c in self.near + self.along + self.relay + list(self.far.values()):
+                c.wait_send()
+            for n in range(PAIRS - 1):
+                self.forward(n).wait_send()
+
+    keys = Spread(kp_hbm, kb, ksend, krecv, kfw)
+    vals = Spread(vp_hbm, vb, vsend, vrecv, vfw)
+    for c in keys.near[:1] + keys.along + vals.near[:1] + keys.near[1:] + vals.near[1:]:
         c.start()
 
     def rows(slot, lo=0, size=CHUNK):
@@ -189,35 +209,36 @@
             m_v[:, at] = jnp.maximum(m_v[:, at], jnp.max(s, axis=0, keepdims=True))
 
     def gather_order(i):
-        return PAIRS - 1 - i - (i == 4).astype(jnp.int32) + (i == 5).astype(jnp.int32)
+        return PAIRS - 1 - i - (i == 5).astype(jnp.int32) + (i == 6).astype(jnp.int32)
+
+    ORDER = (7, 6, 5, 4, 3, 1, 2, 0)
+
+    def take(x, i):
+        for j in range(1, PAIRS):
+            @pl.when(i == j)
+            def _():
+                slot = 2 * ORDER[j] + 1
+                x.arrived(slot)
+                if slot == 13:
+                    for c in x.relay:
+                        c.start()
+                if slot in x.far:
+                    x.far[slot].start()
+                x.forward(ORDER[j]).start()
 
     def score_step(i, carry):
         n = gather_order(i)
-
-        @pl.when(i > 0)
+        take(keys, i)
+
+        @pl.when(i == 3)
         def _():
-            kv_arrived(kb, krecv, ksend, 2 * n + 1)
-            kv_forward(kb, kfw, krecv, n).start()
-
-        @pl.when(i == 1)
-        def _():
-            for c in kv_relay(kb, ksend, krecv):
+            for c in vals.along:
                 c.start()
-            kv_arrived(vb, vrecv, vsend, 13)
-            for c in kv_relay(vb, vsend, vrecv):
+            vals.arrived(13)
+            for c in vals.relay:
                 c.start()
 
-        @pl.when(i == 5)
-        def _():
-            do_own[1].wait_recv()
-            do_relay[0].start()
-            do_own[2].wait_recv()
-            do_relay[1].start()
-            do_own[0].wait_recv()
-            do_relay[2].start()
-            do_relay[3].start()
-
-        kv_arrived(kb, krecv, ksend, 2 * n)
+        keys.forward(n).wait_recv()
         scores_of(n)
         return carry
 
@@ -243,30 +264,49 @@
     output_of(16 * BLK, BLK, True)
     local[1].wait()
 
+    def take_values(i):
+        for j in range(1, PAIRS):
+            @pl.when(i == j)
+            def _():
+                slot = 2 * ORDER[j] + 1
+                if slot not in (13, 11, 9):
+                    vals.arrived(slot)
+                    if slot in vals.far:
+                        vals.far[slot].start()
+                    vals.forward(ORDER[j]).start()
+
     def output_step(i, carry):
         n = gather_order(i)
 
-        @pl.when(i == 1)
+        @pl.when(i == 0)
         def _():
-            kv_forward(vb, vfw, vrecv, n).start()
-
-        @pl.when(i > 1)
+            vals.forward(6).start()
+            for slot in (11, 9):
+                vals.arrived(slot)
+                vals.far[slot].start()
+                vals.forward(slot // 2).start()
+
+        @pl.when(i == 3)
         def _():
-            kv_arrived(vb, vrecv, vsend, 2 * n + 1)
-            kv_forward(vb, vfw, vrecv, n).start()
-
-        @pl.when(i == 1)
-        def _():
-            do_relay[0].wait_recv()
-            do_relay[4].start()
-            do_relay[1].wait_recv()
-            do_relay[5].start()
-
-        kv_arrived(vb, vrecv, vsend, 2 * n)
+            do_own[1].wait_recv()
+            do_relay[0].start()
+            do_own[2].wait_recv()
+            do_relay[1].start()
+            do_own[0].wait_recv()
+            do_relay[2].start()
+            do_relay[3].start()
+
+        take_values(i)
+        vals.forward(n).wait_recv()
         output_of(pair_at(n), PAIR)
         return carry
 
     lax.fori_loop(0, PAIRS, output_step, 0)
+
+    do_relay[0].wait_recv()
+    do_relay[4].start()
+    do_relay[1].wait_recv()
+    do_relay[5].start()
 
     for t in range(ROWS // HD):
         at = pl.ds(t * HD, HD)
@@ -294,35 +334,21 @@
             delta_v[:, at] = jnp.sum(gf * o_t[:, at], axis=0, keepdims=True)
             dop[at, :] = (gf * l_v[:, at]).T.astype(bf16)
 
-    def grads_of(p, at_row, size):
+    def grads_of(at_row, size):
         here = pl.ds(at_row, size)
         vblk = vb[here, :]
-        for c, width in ((0, 256), (256, 256), (512, 128)):
-            at = pl.ds(p * HALF + c, width)
+        for c in range(ROWS // 256):
+            at = pl.ds(c * 256, 256)
             dp = dot(vblk, dot_t[:, at])
-            ds_v[0:size, c:c + width] = (p_v[here, at].astype(f32) * (dp - delta_v[:, at])).astype(bf16)
-        part = pl.ds(p * HALF, HALF)
-        dq_t[:, part] += dot(kt_v[:, here], ds_v[0:size, :])
-        dk = dot(ds_v[0:size, :], qp[part, :])
-        dv = dot(p_v[here, part], dop[part, :])
+            ds_v[0:size, at] = (p_v[here, at].astype(f32) * (dp - delta_v[:, at])).astype(bf16)
+        dq_t[...] += dot(kt_v[:, here], ds_v[0:size, :])
+        dk = dot(ds_v[0:size, :], qp[...])
+        dv = dot(p_v[here, :], dop[...])
         return dk, dv
 
     local[5].wait()
     local[6].wait()
     start_part(0)
-
-    def part_a(n, carry):
-        here = pl.ds(pair_at(n), PAIR)
-        dk, dv = grads_of(0, pair_at(n), PAIR)
-        s_v[here, 0:HD] = dk
-        s_v[here, HD:2 * HD] = dv
-        return carry
-
-    lax.fori_loop(0, PAIRS, part_a, 0)
-    dk, dv = grads_of(0, 16 * BLK, BLK)
-    s_v[OWN, 0:HD] = dk
-    s_v[OWN, HD:2 * HD] = dv
-
     for i in (2, 3, 4, 5):
         do_relay[i].wait_recv()
     start_part(1)
@@ -352,28 +378,36 @@
 
     extras_of = ((), (), (), (0,), (), (2,), (1, 3), (4, 5, 6))
 
-    def part_b(n, carry):
-        dk, dv = grads_of(1, pair_at(n), PAIR)
-        there = pl.ds(pair_at(n), BLK)
-        csend[n, :, 0:HD] = (dk[0:BLK] + s_v[there, 0:HD]).astype(bf16)
-        csend[n, :, HD:2 * HD] = (dv[0:BLK] + s_v[there, HD:2 * HD]).astype(bf16)
+    def pair_grads(n):
+        dk, dv = grads_of(pair_at(n), PAIR)
+        csend[n, :, 0:HD] = dk[0:BLK].astype(bf16)
+        csend[n, :, HD:2 * HD] = dv[0:BLK].astype(bf16)
         core_copy(n).start()
-        s_v[own_half(n), 0:HD] += dk[BLK:]
-        s_v[own_half(n), HD:2 * HD] += dv[BLK:]
-
-        for j in range(7):
+        s_v[own_half(n), 0:HD] = dk[BLK:]
+        s_v[own_half(n), HD:2 * HD] = dv[BLK:]
+
+    def grad_step(n, carry):
+        pair_grads(n)
+
+        @pl.when(n == PAIRS - 2)
+        def _():
+            dk, dv = grads_of(16 * BLK, BLK)
+            dvn_ref[...] = dv.astype(bf16)
+            dkn_ref[...] = (dk * cos_v[...] - pltpu.roll(dk, HD // 2, 1) * sin_v[...]).astype(bf16)
+            core_copy(6).wait_recv()
+
+        for j in range(6):
             @pl.when(n == j + 1)
             def _():
                 core_copy(j).wait_recv()
                 finish(j, j, extras_of[j])
+
+        @pl.when(n == PAIRS - 2)
+        def _():
+            finish(6, 6, extras_of[6])
         return carry
 
-    lax.fori_loop(0, PAIRS, part_b, 0)
-
-    dk, dv = grads_of(1, 16 * BLK, BLK)
-    dk = dk + s_v[OWN, 0:HD]
-    dvn_ref[...] = (dv + s_v[OWN, HD:2 * HD]).astype(bf16)
-    dkn_ref[...] = (dk * cos_v[...] - pltpu.roll(dk, HD // 2, 1) * sin_v[...]).astype(bf16)
+    lax.fori_loop(0, PAIRS, grad_step, 0)
 
     for p in range(2):
         for h in range(HEADS):
@@ -389,11 +423,8 @@
     core_copy(7).wait_recv()
     finish(7, 7, extras_of[7])
 
-    for src, buf, ssem, fsem, rsem in ((kp_hbm, kb, ksend, kfw, krecv), (vp_hbm, vb, vsend, vfw, vrecv)):
-        for c in kv_own(src, buf, ssem, rsem) + kv_relay(buf, ssem, rsem):
-            c.wait_send()
-        for n in range(PAIRS - 1):
-            kv_forward(buf, fsem, rsem, n).wait_send()
+    keys.wait_send()
+    vals.wait_send()
     for c in do_own + do_relay:
         c.wait_send()
     for n in range(PAIRS):
@@ -403,12 +434,8 @@
 
 
 def hand_over(*refs):
-    sources, results, sems = refs[:5], refs[5:10], refs[10]
-    copies = [pltpu.make_async_copy(a, b, sems.at[i]) for i, (a, b) in enumerate(zip(sources, results))]
-    for c in copies:
-        c.start()
-    for c in copies:
-        c.wait()
+    for source, result in zip(refs[:5], refs[5:]):
+        result[...] = source[...]
 
 
 def local(out_grad, out_weight, queries, keys_new, values_new, keys_prompt, values_prompt, offsets):
@@ -451,19 +478,19 @@
             pltpu.VMEM((1, ROWS), f32),
             pltpu.VMEM((SEQ, HD), f32),
             pltpu.VMEM((SEQ, HD), f32),
-            pltpu.VMEM((PAIR, HALF), bf16),
+            pltpu.VMEM((PAIR, ROWS), bf16),
             pltpu.VMEM((HEADS * HD, HD), f32),
             pltpu.VMEM((PAIRS, BLK, 2 * HD), bf16),
             pltpu.VMEM((PAIRS, BLK, 2 * HD), bf16),
             pltpu.VMEM((7, BLK, 2 * HD), bf16),
             pltpu.VMEM((7, BLK, 2 * HD), bf16),
             dma((7,)),
-            dma((8,)),
-            dma((8,)),
+            dma((10,)),
+            dma((10,)),
             dma((7,)),
             dma((7,)),
-            dma((16,)),
-            dma((16,)),
+            dma((18,)),
+            dma((18,)),
             dma((9,)),
             dma((9,)),
             dma((8,)),
@@ -489,9 +516,8 @@
     dq, dkn, dvn, dkp, dvp = pl.pallas_call(
         hand_over,
         out_shape=tuple(jax.ShapeDtypeStruct(g.shape, g.dtype) for g in grads),
-        in_specs=[any_spec] * 5,
-        out_specs=(any_spec,) * 5,
-        scratch_shapes=[dma((5,))],
+        in_specs=[vmem] * 5,
+        out_specs=(vmem,) * 5,
         name="hand_over",
     )(*grads)
     grad_queries = jnp.transpose(dq.reshape(HEADS, SEQ, HD), (1, 0, 2))[None, :, None]

time: 89.5 us -> 69 us (0.77)
  Pallas kernels: 88.1 us -> 67.5 us
    pallas_call x1, Pallas kernels: 19 us -> 1.86 us  [local(): pl.pallas_call(hand_over, out_shape=tuple((jax.ShapeDtypeStruct(g.shape,...]
    pallas_call x1, Pallas kernels: 69.1 us -> 65.7 us  [local(): pl.pallas_call(kernel, out_shape=(jax.ShapeDtypeStruct((ROWS, HD), bf16),...]
where the time goes in v3:
time: 69 us; the launch traced here: 68.8 us
  Pallas kernels  67.5 us (98%)
  between operations  1.29 us (2%)
    pallas_call x1, Pallas kernels, local(): pl.pallas_call(kernel, out_shape=(jax.ShapeDtypeStruct((ROWS, HD), bf16),...  65.7 us
    pallas_call x1, Pallas kernels, local(): pl.pallas_call(hand_over, out_shape=tuple((jax.ShapeDtypeStruct(g.shape,...  1.86 us

profile of v3, /device:TPU:1, one launch (start us, length us, event | category | flops | bytes accessed | tf_op | source)
XLA Modules:
  0.0 68.8 jit_solution(3528725554322794276)
XLA Ops:
  1.3 65.7 %attention_backward.1 = (bf16[1280,128]{1,0:T(8,128)(2,1)}, bf16[256,128]{1,0:T(8,128)(2,1)}, bf16[256,128]{1,0:T(8,128)(2,1)}, bf16[256,128]{1,0:T(8,128)(2,1)}, bf16[256,128]{1,0:T(8,128)(2,1)}) custom-call(bf16[32,5120]{1,0:T(8,128)(2,1)} %bitcast.21, bf16[640,5120]{1,0:T(8,128)(2,1)} %bitcast.20, bf16[1280,128]{1,0:T(8,128)(2,1)} %bitcast.22, ...), custom_call_target="tpu_custom_call" | custom-call | tf_op jit(solution)/shard_map/attention_backward/pallas_call | solution.py:449
  67.0 1.9 %hand_over.1 = (bf16[1280,128]{1,0:T(8,128)(2,1)}, bf16[256,128]{1,0:T(8,128)(2,1)}, bf16[256,128]{1,0:T(8,128)(2,1)}, bf16[256,128]{1,0:T(8,128)(2,1)}, bf16[256,128]{1,0:T(8,128)(2,1)}) custom-call(bf16[1280,128]{1,0:T(8,128)(2,1)} %get-tuple-element.15.refs_0_, bf16[256,128]{1,0:T(8,128)(2,1)} %get-tuple-element.16.refs_1_, ...), custom_call_target="tpu_custom_call" | custom-call | tf_op jit(solution)/shard_map/hand_over/pallas_call | solution.py:516

commit v4 on v3

--- a/solution.py
+++ b/solution.py
@@ -40,7 +40,7 @@
     og_hbm, w_hbm, q_hbm, kn_hbm, vn_hbm, kp_hbm, vp_hbm, off_ref, freq_ref,
     dq_ref, dkn_ref, dvn_ref, dkp_ref, dvp_ref,
     w_v, do_v, kb, vb, kt_v, q_v, kn_v, qt, qp, dot_t, dop, s_v, p_v, o_t, dq_t, m_v, l_v, delta_v,
-    cos_v, sin_v, ds_v, ag_v, csend, crecv, zs, zr,
+    cos_v, sin_v, ag_v, csend, crecv, zs, zr,
     lsem, ksend, vsend, kfw, vfw, krecv, vrecv, dsend, drecv, cs_sem, cr_sem, zs_sem, zr_sem,
 ):
     roll = lax.axis_index("roll")
@@ -54,11 +54,11 @@
         return (r, k)
 
     core, yhp = dev(dc=1), dev(dyh=1)
-    zp, zm = dev(dz=1), dev(dz=3)
+    zp, zm, z2 = dev(dz=1), dev(dz=3), dev(dz=2)
     ylp, xp, xm = dev(dyl=1), dev(dx=1), dev(dx=3)
 
     barrier = pltpu.get_barrier_semaphore()
-    for d in (core, yhp, zp, zm, ylp, xp, xm):
+    for d in (core, yhp, zp, zm, z2, ylp, xp, xm):
         pl.semaphore_signal(barrier, 1, device_id=d, device_id_type=MESH)
 
     local = [
@@ -80,29 +80,25 @@
     sin_a = jnp.sin(angle)
     sin_v[...] = jnp.where(lane < HD // 2, -sin_a, sin_a)
 
-    pl.semaphore_wait(barrier, 7)
+    pl.semaphore_wait(barrier, 8)
 
     def remote(src, dst, ssem, rsem, d):
         return pltpu.make_async_remote_copy(
             src_ref=src, dst_ref=dst, send_sem=ssem, recv_sem=rsem, device_id=d, device_id_type=MESH
         )
 
-    def blk(buf, slot, lo=0, size=BLK):
-        return buf.at[pl.ds(slot * BLK + lo, size)]
+    def blk(buf, slot):
+        return buf.at[pl.ds(slot * BLK, BLK)]
 
     class Spread:
         def __init__(self, src, buf, send, recv, fsend):
-            self.src, self.buf, self.send, self.recv, self.fsend = src, buf, send, recv, fsend
-            mid = BLK // 2
-            self.near = [self.hop(src, 13, 0, yhp), self.hop(src, 14, 1, core)]
-            self.along = [self.hop(src, 9, 2, zp), self.hop(src, 11, 3, zm)]
-            self.relay = [self.hop(blk(buf, 13), 7, 4, zp), self.hop(blk(buf, 13), 3, 5, zm)]
-            self.far = {
-                9: remote(blk(buf, 9, 0, mid), blk(buf, 5, 0, mid), send.at[6], recv.at[5], zp),
-                11: remote(blk(buf, 11, mid, mid), blk(buf, 5, mid, mid), send.at[7], recv.at[16], zm),
-                7: remote(blk(buf, 7, 0, mid), blk(buf, 1, 0, mid), send.at[8], recv.at[1], zp),
-                3: remote(blk(buf, 3, mid, mid), blk(buf, 1, mid, mid), send.at[9], recv.at[17], zm),
-            }
+            self.buf, self.send, self.recv, self.fsend = buf, send, recv, fsend
+            self.own = [
+                self.hop(src, s, i, d) for i, (s, d) in enumerate(((13, yhp), (11, zp), (9, zm), (7, z2), (14, core)))
+            ]
+            self.relay = [
+                self.hop(blk(buf, 13), s, 5 + i, d) for i, (s, d) in enumerate(((5, zp), (3, zm), (1, z2)))
+            ]
 
         def hop(self, src, slot, i, d):
             return remote(src, blk(self.buf, slot), self.send.at[i], self.recv.at[slot], d)
@@ -112,25 +108,20 @@
                 blk(self.buf, 2 * n + 1), blk(self.buf, 2 * n), self.fsend.at[n], self.recv.at[2 * n], core
             )
 
-        def arrived(self, slot):
-            if slot == 5:
-                self.far[9].wait_recv()
-                self.far[11].wait_recv()
-            elif slot == 1:
-                self.far[7].wait_recv()
-                self.far[3].wait_recv()
-            else:
-                self.hop(blk(self.buf, slot), slot, 0, core).wait_recv()
+        def take(self, n):
+            slot = 2 * n + 1
+            self.hop(blk(self.buf, slot), slot, 0, core).wait_recv()
+            self.forward(n).start()
 
         def wait_send(self):
-            for c in self.near + self.along + self.relay + list(self.far.values()):
+            for c in self.own + self.relay:
                 c.wait_send()
             for n in range(PAIRS - 1):
                 self.forward(n).wait_send()
 
     keys = Spread(kp_hbm, kb, ksend, krecv, kfw)
     vals = Spread(vp_hbm, vb, vsend, vrecv, vfw)
-    for c in keys.near[:1] + keys.along + vals.near[:1] + keys.near[1:] + vals.near[1:]:
+    for c in keys.own[:1] + vals.own[:1] + keys.own[1:] + vals.own[1:]:
         c.start()
 
     def rows(slot, lo=0, size=CHUNK):
@@ -138,8 +129,10 @@
 
     do_own = [
         remote(og_hbm, rows(1), dsend.at[0], drecv.at[0], ylp),
-        remote(og_hbm, rows(3), dsend.at[1], drecv.at[1], xp),
-        remote(og_hbm, rows(2), dsend.at[2], drecv.at[2], xm),
+        remote(og_hbm.at[pl.ds(0, 16)], rows(3, 0, 16), dsend.at[1], drecv.at[1], xp),
+        remote(og_hbm.at[pl.ds(16, 16)], rows(2, 16, 16), dsend.at[2], drecv.at[2], xm),
+        remote(og_hbm.at[pl.ds(16, 16)], rows(3, 16, 16), dsend.at[9], drecv.at[9], xp),
+        remote(og_hbm.at[pl.ds(0, 16)], rows(2, 0, 16), dsend.at[10], drecv.at[10], xm),
     ]
     do_relay = [
         remote(rows(3, 0, 16), rows(4, 0, 16), dsend.at[3], drecv.at[3], xp),
@@ -208,35 +201,34 @@
             s_v[here, at] = s
             m_v[:, at] = jnp.maximum(m_v[:, at], jnp.max(s, axis=0, keepdims=True))
 
-    def gather_order(i):
-        return PAIRS - 1 - i - (i == 5).astype(jnp.int32) + (i == 6).astype(jnp.int32)
-
-    ORDER = (7, 6, 5, 4, 3, 1, 2, 0)
-
-    def take(x, i):
-        for j in range(1, PAIRS):
+    def score_step(i, carry):
+        n = PAIRS - 1 - i
+
+        @pl.when(i == 1)
+        def _():
+            keys.take(6)
+            for c in keys.relay:
+                c.start()
+            vals.take(6)
+            for c in vals.relay:
+                c.start()
+            do_own[1].wait_recv()
+            do_relay[0].start()
+            do_own[2].wait_recv()
+            do_relay[1].start()
+            for j in (5, 4, 3):
+                keys.take(j)
+
+        for j, ahead in ((4, 2), (5, 1), (6, 0)):
             @pl.when(i == j)
             def _():
-                slot = 2 * ORDER[j] + 1
-                x.arrived(slot)
-                if slot == 13:
-                    for c in x.relay:
-                        c.start()
-                if slot in x.far:
-                    x.far[slot].start()
-                x.forward(ORDER[j]).start()
-
-    def score_step(i, carry):
-        n = gather_order(i)
-        take(keys, i)
-
-        @pl.when(i == 3)
+                keys.take(ahead)
+
+        @pl.when(i == 6)
         def _():
-            for c in vals.along:
-                c.start()
-            vals.arrived(13)
-            for c in vals.relay:
-                c.start()
+            do_own[0].wait_recv()
+            do_relay[2].start()
+            do_relay[3].start()
 
         keys.forward(n).wait_recv()
         scores_of(n)
@@ -264,49 +256,31 @@
     output_of(16 * BLK, BLK, True)
     local[1].wait()
 
-    def take_values(i):
-        for j in range(1, PAIRS):
+    def output_step(i, carry):
+        n = PAIRS - 1 - i
+
+        @pl.when(i == 0)
+        def _():
+            for j in (5, 4, 3):
+                vals.take(j)
+
+        for j, ahead in ((3, 2), (4, 1), (5, 0)):
             @pl.when(i == j)
             def _():
-                slot = 2 * ORDER[j] + 1
-                if slot not in (13, 11, 9):
-                    vals.arrived(slot)
-                    if slot in vals.far:
-                        vals.far[slot].start()
-                    vals.forward(ORDER[j]).start()
-
-    def output_step(i, carry):
-        n = gather_order(i)
-
-        @pl.when(i == 0)
+                vals.take(ahead)
+
+        @pl.when(i == 1)
         def _():
-            vals.forward(6).start()
-            for slot in (11, 9):
-                vals.arrived(slot)
-                vals.far[slot].start()
-                vals.forward(slot // 2).start()
-
-        @pl.when(i == 3)
-        def _():
-            do_own[1].wait_recv()
-            do_relay[0].start()
-            do_own[2].wait_recv()
-            do_relay[1].start()
-            do_own[0].wait_recv()
-            do_relay[2].start()
-            do_relay[3].start()
-
-        take_values(i)
+            do_relay[0].wait_recv()
+            do_relay[4].start()
+            do_relay[1].wait_recv()
+            do_relay[5].start()
+
         vals.forward(n).wait_recv()
         output_of(pair_at(n), PAIR)
         return carry
 
     lax.fori_loop(0, PAIRS, output_step, 0)
-
-    do_relay[0].wait_recv()
-    do_relay[4].start()
-    do_relay[1].wait_recv()
-    do_relay[5].start()
 
     for t in range(ROWS // HD):
         at = pl.ds(t * HD, HD)
@@ -314,8 +288,6 @@
         l_v[:, at] = inv
         o_t[:, at] *= inv
         qp[at, :] = (qt[:, at].astype(f32) * (inv * SCALE)).T.astype(bf16)
-
-    dq_t[...] = jnp.zeros_like(dq_t)
 
     def start_part(p):
         ag_v[...] = jnp.zeros_like(ag_v)
@@ -337,17 +309,18 @@
     def grads_of(at_row, size):
         here = pl.ds(at_row, size)
         vblk = vb[here, :]
+        dv = dot(p_v[here, :], dop[...])
         for c in range(ROWS // 256):
             at = pl.ds(c * 256, 256)
             dp = dot(vblk, dot_t[:, at])
-            ds_v[0:size, at] = (p_v[here, at].astype(f32) * (dp - delta_v[:, at])).astype(bf16)
-        dq_t[...] += dot(kt_v[:, here], ds_v[0:size, :])
-        dk = dot(ds_v[0:size, :], qp[...])
-        dv = dot(p_v[here, :], dop[...])
+            p_v[here, at] = (p_v[here, at].astype(f32) * (dp - delta_v[:, at])).astype(bf16)
+        dk = dot(p_v[here, :], qp[...])
         return dk, dv
 
     local[5].wait()
     local[6].wait()
+    do_own[3].wait_recv()
+    do_own[4].wait_recv()
     start_part(0)
     for i in (2, 3, 4, 5):
         do_relay[i].wait_recv()
@@ -356,7 +329,7 @@
     def core_copy(n):
         return remote(csend.at[n], crecv.at[n], cs_sem.at[n], cr_sem.at[n], core)
 
-    z_dest = (zm, zp, zp, zm, zm, zp, yhp)
+    z_dest = (z2, zp, zm, z2, zp, zm, yhp)
 
     def z_copy(j):
         return remote(zs.at[j], zr.at[j], zs_sem.at[j], zr_sem.at[j], z_dest[j])
@@ -376,7 +349,7 @@
             dkp_ref[...] = total[:, 0:HD].astype(bf16)
             dvp_ref[...] = total[:, HD:2 * HD].astype(bf16)
 
-    extras_of = ((), (), (), (0,), (), (2,), (1, 3), (4, 5, 6))
+    extras_of = ((), (), (), (), (), (), (0, 1, 2), (3, 4, 5, 6))
 
     def pair_grads(n):
         dk, dv = grads_of(pair_at(n), PAIR)
@@ -389,26 +362,28 @@
     def grad_step(n, carry):
         pair_grads(n)
 
-        @pl.when(n == PAIRS - 2)
-        def _():
-            dk, dv = grads_of(16 * BLK, BLK)
-            dvn_ref[...] = dv.astype(bf16)
-            dkn_ref[...] = (dk * cos_v[...] - pltpu.roll(dk, HD // 2, 1) * sin_v[...]).astype(bf16)
-            core_copy(6).wait_recv()
-
         for j in range(6):
             @pl.when(n == j + 1)
             def _():
                 core_copy(j).wait_recv()
                 finish(j, j, extras_of[j])
 
-        @pl.when(n == PAIRS - 2)
-        def _():
-            finish(6, 6, extras_of[6])
         return carry
 
     lax.fori_loop(0, PAIRS, grad_step, 0)
 
+    dk, dv = grads_of(16 * BLK, BLK)
+    dvn_ref[...] = dv.astype(bf16)
+    dkn_ref[...] = (dk * cos_v[...] - pltpu.roll(dk, HD // 2, 1) * sin_v[...]).astype(bf16)
+    core_copy(6).wait_recv()
+    finish(6, 6, extras_of[6])
+
+    def query_step(c, carry):
+        at = pl.ds(pl.multiple_of(c * 256, 256), 256)
+        dq_t[:, at] = dot(kt_v[...], p_v[:, at])
+        return carry
+
+    lax.fori_loop(0, ROWS // 256, query_step, 0)
     for p in range(2):
         for h in range(HEADS):
             at = pl.ds((p * HEADS + h) * HD, HD)
@@ -478,21 +453,20 @@
             pltpu.VMEM((1, ROWS), f32),
             pltpu.VMEM((SEQ, HD), f32),
             pltpu.VMEM((SEQ, HD), f32),
-            pltpu.VMEM((PAIR, ROWS), bf16),
             pltpu.VMEM((HEADS * HD, HD), f32),
             pltpu.VMEM((PAIRS, BLK, 2 * HD), bf16),
             pltpu.VMEM((PAIRS, BLK, 2 * HD), bf16),
             pltpu.VMEM((7, BLK, 2 * HD), bf16),
             pltpu.VMEM((7, BLK, 2 * HD), bf16),
             dma((7,)),
-            dma((10,)),
-            dma((10,)),
+            dma((8,)),
+            dma((8,)),
             dma((7,)),
             dma((7,)),
-            dma((18,)),
-            dma((18,)),
-            dma((9,)),
-            dma((9,)),
+            dma((16,)),
+            dma((16,)),
+            dma((11,)),
+            dma((11,)),
             dma((8,)),
             dma((8,)),
             dma((7,)),

time: 69 us -> 59.8 us (0.87)
  Pallas kernels: 67.5 us -> 58.3 us
    pallas_call x1, Pallas kernels: 65.7 us -> 56.4 us  [local(): pl.pallas_call(kernel, out_shape=(jax.ShapeDtypeStruct((ROWS, HD), bf16),...]
where the time goes in v4:
time: 59.8 us; the launch traced here: 59.6 us
  Pallas kernels  58.3 us (97%)
  between operations  1.29 us (2%)
    pallas_call x1, Pallas kernels, local(): pl.pallas_call(kernel, out_shape=(jax.ShapeDtypeStruct((ROWS, HD), bf16),...  56.4 us
    pallas_call x1, Pallas kernels, local(): pl.pallas_call(hand_over, out_shape=tuple((jax.ShapeDtypeStruct(g.shape,...  1.86 us

profile of v4, /device:TPU:1, one launch (start us, length us, event | category | flops | bytes accessed | tf_op | source)
XLA Modules:
  0.0 59.6 jit_solution(1538195769095021690)
XLA Ops:
  1.3 56.4 %attention_backward.1 = (bf16[1280,128]{1,0:T(8,128)(2,1)}, bf16[256,128]{1,0:T(8,128)(2,1)}, bf16[256,128]{1,0:T(8,128)(2,1)}, bf16[256,128]{1,0:T(8,128)(2,1)}, bf16[256,128]{1,0:T(8,128)(2,1)}) custom-call(bf16[32,5120]{1,0:T(8,128)(2,1)} %bitcast.21, bf16[640,5120]{1,0:T(8,128)(2,1)} %bitcast.20, bf16[1280,128]{1,0:T(8,128)(2,1)} %bitcast.22, ...), custom_call_target="tpu_custom_call" | custom-call | tf_op jit(solution)/shard_map/attention_backward/pallas_call | solution.py:424
  57.7 1.9 %hand_over.1 = (bf16[1280,128]{1,0:T(8,128)(2,1)}, bf16[256,128]{1,0:T(8,128)(2,1)}, bf16[256,128]{1,0:T(8,128)(2,1)}, bf16[256,128]{1,0:T(8,128)(2,1)}, bf16[256,128]{1,0:T(8,128)(2,1)}) custom-call(bf16[1280,128]{1,0:T(8,128)(2,1)} %get-tuple-element.15.refs_0_, bf16[256,128]{1,0:T(8,128)(2,1)} %get-tuple-element.16.refs_1_, ...), custom_call_target="tpu_custom_call" | custom-call | tf_op jit(solution)/shard_map/hand_over/pallas_call | solution.py:490

commit v5 on v4

--- a/solution.py
+++ b/solution.py
@@ -40,7 +40,7 @@
     og_hbm, w_hbm, q_hbm, kn_hbm, vn_hbm, kp_hbm, vp_hbm, off_ref, freq_ref,
     dq_ref, dkn_ref, dvn_ref, dkp_ref, dvp_ref,
     w_v, do_v, kb, vb, kt_v, q_v, kn_v, qt, qp, dot_t, dop, s_v, p_v, o_t, dq_t, m_v, l_v, delta_v,
-    cos_v, sin_v, ag_v, csend, crecv, zs, zr,
+    cos_v, sin_v, ds_v, ag_v, csend, crecv, zs, zr,
     lsem, ksend, vsend, kfw, vfw, krecv, vrecv, dsend, drecv, cs_sem, cr_sem, zs_sem, zr_sem,
 ):
     roll = lax.axis_index("roll")
@@ -124,8 +124,10 @@
     for c in keys.own[:1] + vals.own[:1] + keys.own[1:] + vals.own[1:]:
         c.start()
 
-    def rows(slot, lo=0, size=CHUNK):
-        return do_v.at[pl.ds(slot * CHUNK + lo, size)]
+    mid = WIDTH // 2
+
+    def rows(slot, lo=0, size=CHUNK, col=0, width=WIDTH):
+        return do_v.at[pl.ds(slot * CHUNK + lo, size), pl.ds(col, width)]
 
     do_own = [
         remote(og_hbm, rows(1), dsend.at[0], drecv.at[0], ylp),
@@ -137,10 +139,14 @@
     do_relay = [
         remote(rows(3, 0, 16), rows(4, 0, 16), dsend.at[3], drecv.at[3], xp),
         remote(rows(2, 16, 16), rows(4, 16, 16), dsend.at[4], drecv.at[4], xm),
-        remote(rows(1), rows(6), dsend.at[5], drecv.at[5], xp),
-        remote(rows(1), rows(5), dsend.at[6], drecv.at[6], xm),
-        remote(rows(4, 0, 16), rows(7, 0, 16), dsend.at[7], drecv.at[7], ylp),
-        remote(rows(4, 16, 16), rows(7, 16, 16), dsend.at[8], drecv.at[8], ylp),
+    ]
+    pair_relay = [
+        remote(rows(1, 0, CHUNK, col, mid), rows(slot, 0, CHUNK, col, mid), dsend.at[i], drecv.at[i], d)
+        for i, col, slot, d in ((5, 0, 6, xp), (6, 0, 5, xm), (7, mid, 6, xp), (8, mid, 5, xm))
+    ]
+    last_relay = [
+        remote(rows(4, lo, 16, col, mid), rows(7, lo, 16, col, mid), dsend.at[i], drecv.at[i], ylp)
+        for i, col, lo in ((11, 0, 0), (12, 0, 16), (13, mid, 0), (14, mid, 16))
     ]
     for c in do_own:
         c.start()
@@ -201,6 +207,18 @@
             s_v[here, at] = s
             m_v[:, at] = jnp.maximum(m_v[:, at], jnp.max(s, axis=0, keepdims=True))
 
+    def project(p, part):
+        tokens_at = slice(p * HD, (p + 1) * HD)
+
+        def step(i, carry):
+            at = pl.ds(pl.multiple_of(part * mid + i * 1280, 1280), 1280)
+            ag_v[p] += dot_nt(w_v[:, at], do_v[tokens_at, at])
+            return carry
+
+        lax.fori_loop(0, mid // 1280, step, 0)
+
+    ag_v[...] = jnp.zeros_like(ag_v)
+
     def score_step(i, carry):
         n = PAIRS - 1 - i
 
@@ -227,8 +245,14 @@
         @pl.when(i == 6)
         def _():
             do_own[0].wait_recv()
-            do_relay[2].start()
-            do_relay[3].start()
+            for c in pair_relay:
+                c.start()
+            do_own[3].wait_recv()
+            do_own[4].wait_recv()
+            local[5].wait()
+            local[6].wait()
+            project(0, 0)
+            project(0, 1)
 
         keys.forward(n).wait_recv()
         scores_of(n)
@@ -271,10 +295,10 @@
 
         @pl.when(i == 1)
         def _():
-            do_relay[0].wait_recv()
-            do_relay[4].start()
-            do_relay[1].wait_recv()
-            do_relay[5].start()
+            for c in do_relay:
+                c.wait_recv()
+            for c in last_relay:
+                c.start()
 
         vals.forward(n).wait_recv()
         output_of(pair_at(n), PAIR)
@@ -289,42 +313,34 @@
         o_t[:, at] *= inv
         qp[at, :] = (qt[:, at].astype(f32) * (inv * SCALE)).T.astype(bf16)
 
-    def start_part(p):
-        ag_v[...] = jnp.zeros_like(ag_v)
-
-        def ag_step(i, carry):
-            at = pl.ds(pl.multiple_of(i * 1024, 1024), 1024)
-            ag_v[...] += dot_nt(w_v[:, at], do_v[p * HD:(p + 1) * HD, at])
-            return carry
-
-        lax.fori_loop(0, WIDTH // 1024, ag_step, 0)
+    def row_terms(p):
         for h in range(HEADS):
             at = pl.ds((p * HEADS + h) * HD, HD)
-            g = ag_v[h * HD:(h + 1) * HD, :].astype(bf16)
+            g = ag_v[p, h * HD:(h + 1) * HD, :].astype(bf16)
             dot_t[:, at] = g
             gf = g.astype(f32)
             delta_v[:, at] = jnp.sum(gf * o_t[:, at], axis=0, keepdims=True)
             dop[at, :] = (gf * l_v[:, at]).T.astype(bf16)
 
-    def grads_of(at_row, size):
+    def grads_of(at_row, size, ds, col):
         here = pl.ds(at_row, size)
         vblk = vb[here, :]
-        dv = dot(p_v[here, :], dop[...])
         for c in range(ROWS // 256):
             at = pl.ds(c * 256, 256)
             dp = dot(vblk, dot_t[:, at])
-            p_v[here, at] = (p_v[here, at].astype(f32) * (dp - delta_v[:, at])).astype(bf16)
-        dk = dot(p_v[here, :], qp[...])
+            ds[:, pl.ds(col + c * 256, 256)] = (p_v[here, at].astype(f32) * (dp - delta_v[:, at])).astype(bf16)
+        dk = dot(ds[:, pl.ds(col, ROWS)], qp[...])
+        dv = dot(p_v[here, :], dop[...])
         return dk, dv
 
-    local[5].wait()
-    local[6].wait()
-    do_own[3].wait_recv()
-    do_own[4].wait_recv()
-    start_part(0)
-    for i in (2, 3, 4, 5):
-        do_relay[i].wait_recv()
-    start_part(1)
+    row_terms(0)
+    for c in (pair_relay[0], pair_relay[1], last_relay[0], last_relay[1]):
+        c.wait_recv()
+    project(1, 0)
+    for c in (pair_relay[2], pair_relay[3], last_relay[2], last_relay[3]):
+        c.wait_recv()
+    project(1, 1)
+    row_terms(1)
 
     def core_copy(n):
         return remote(csend.at[n], crecv.at[n], cs_sem.at[n], cr_sem.at[n], core)
@@ -351,28 +367,33 @@
 
     extras_of = ((), (), (), (), (), (), (0, 1, 2), (3, 4, 5, 6))
 
-    def pair_grads(n):
-        dk, dv = grads_of(pair_at(n), PAIR)
+    def pair_grads(n, ds, col):
+        dk, dv = grads_of(pair_at(n), PAIR, ds, col)
         csend[n, :, 0:HD] = dk[0:BLK].astype(bf16)
         csend[n, :, HD:2 * HD] = dv[0:BLK].astype(bf16)
         core_copy(n).start()
         s_v[own_half(n), 0:HD] = dk[BLK:]
         s_v[own_half(n), HD:2 * HD] = dv[BLK:]
 
-    def grad_step(n, carry):
-        pair_grads(n)
-
         for j in range(6):
             @pl.when(n == j + 1)
             def _():
                 core_copy(j).wait_recv()
                 finish(j, j, extras_of[j])
 
+    def first_step(n, carry):
+        pair_grads(n, w_v.at[pl.ds(0, PAIR)], pl.multiple_of(n * ROWS, ROWS))
         return carry
 
-    lax.fori_loop(0, PAIRS, grad_step, 0)
-
-    dk, dv = grads_of(16 * BLK, BLK)
+    lax.fori_loop(0, PAIRS // 2, first_step, 0)
+
+    def second_step(n, carry):
+        pair_grads(n, ds_v.at[pl.ds(pl.multiple_of((n - PAIRS // 2) * PAIR, PAIR), PAIR)], 0)
+        return carry
+
+    lax.fori_loop(PAIRS // 2, PAIRS, second_step, 0)
+
+    dk, dv = grads_of(16 * BLK, BLK, ds_v.at[pl.ds(8 * BLK, BLK)], 0)
     dvn_ref[...] = dv.astype(bf16)
     dkn_ref[...] = (dk * cos_v[...] - pltpu.roll(dk, HD // 2, 1) * sin_v[...]).astype(bf16)
     core_copy(6).wait_recv()
@@ -380,7 +401,12 @@
 
     def query_step(c, carry):
         at = pl.ds(pl.multiple_of(c * 256, 256), 256)
-        dq_t[:, at] = dot(kt_v[...], p_v[:, at])
+        total = dot(kt_v[:, 8 * BLK:], ds_v[:, at])
+        for n in range(PAIRS // 2):
+            total += dot(
+                kt_v[:, n * PAIR:(n + 1) * PAIR], w_v[0:PAIR, pl.ds(pl.multiple_of(n * ROWS + c * 256, 256), 256)]
+            )
+        dq_t[:, at] = total
         return carry
 
     lax.fori_loop(0, ROWS // 256, query_step, 0)
@@ -400,7 +426,7 @@
 
     keys.wait_send()
     vals.wait_send()
-    for c in do_own + do_relay:
+    for c in do_own + do_relay + pair_relay + last_relay:
         c.wait_send()
     for n in range(PAIRS):
         core_copy(n).wait_send()
@@ -453,7 +479,8 @@
             pltpu.VMEM((1, ROWS), f32),
             pltpu.VMEM((SEQ, HD), f32),
             pltpu.VMEM((SEQ, HD), f32),
-            pltpu.VMEM((HEADS * HD, HD), f32),
+            pltpu.VMEM((9 * BLK, ROWS), bf16),
+            pltpu.VMEM((2, HEADS * HD, HD), f32),
             pltpu.VMEM((PAIRS, BLK, 2 * HD), bf16),
             pltpu.VMEM((PAIRS, BLK, 2 * HD), bf16),
             pltpu.VMEM((7, BLK, 2 * HD), bf16),
@@ -465,8 +492,8 @@
             dma((7,)),
             dma((16,)),
             dma((16,)),
-            dma((11,)),
-            dma((11,)),
+            dma((15,)),
+            dma((15,)),
             dma((8,)),
             dma((8,)),
             dma((7,)),

time: 59.8 us -> 59 us (0.987)
  Pallas kernels: 58.3 us -> 57.5 us
    pallas_call x1, Pallas kernels: 56.4 us -> 55.7 us  [local(): pl.pallas_call(kernel, out_shape=(jax.ShapeDtypeStruct((ROWS, HD), bf16),...]
where the time goes in v5:
time: 59 us; the launch traced here: 58.8 us
  Pallas kernels  57.5 us (97%)
  between operations  1.29 us (2%)
    pallas_call x1, Pallas kernels, local(): pl.pallas_call(kernel, out_shape=(jax.ShapeDtypeStruct((ROWS, HD), bf16),...  55.7 us
    pallas_call x1, Pallas kernels, local(): pl.pallas_call(hand_over, out_shape=tuple((jax.ShapeDtypeStruct(g.shape,...  1.86 us

profile of v5, /device:TPU:1, one launch (start us, length us, event | category | flops | bytes accessed | tf_op | source)
XLA Modules:
  0.0 58.8 jit_solution(9194040811261972286)
XLA Ops:
  1.3 55.7 %attention_backward.1 = (bf16[1280,128]{1,0:T(8,128)(2,1)}, bf16[256,128]{1,0:T(8,128)(2,1)}, bf16[256,128]{1,0:T(8,128)(2,1)}, bf16[256,128]{1,0:T(8,128)(2,1)}, bf16[256,128]{1,0:T(8,128)(2,1)}) custom-call(bf16[32,5120]{1,0:T(8,128)(2,1)} %bitcast.21, bf16[640,5120]{1,0:T(8,128)(2,1)} %bitcast.20, bf16[1280,128]{1,0:T(8,128)(2,1)} %bitcast.22, ...), custom_call_target="tpu_custom_call" | custom-call | tf_op jit(solution)/shard_map/attention_backward/pallas_call | solution.py:450
  56.9 1.9 %hand_over.1 = (bf16[1280,128]{1,0:T(8,128)(2,1)}, bf16[256,128]{1,0:T(8,128)(2,1)}, bf16[256,128]{1,0:T(8,128)(2,1)}, bf16[256,128]{1,0:T(8,128)(2,1)}, bf16[256,128]{1,0:T(8,128)(2,1)}) custom-call(bf16[1280,128]{1,0:T(8,128)(2,1)} %get-tuple-element.15.refs_0_, bf16[256,128]{1,0:T(8,128)(2,1)} %get-tuple-element.16.refs_1_, ...), custom_call_target="tpu_custom_call" | custom-call | tf_op jit(solution)/shard_map/hand_over/pallas_call | solution.py:517

commit v6 on v5

--- a/solution.py
+++ b/solution.py
@@ -322,16 +322,17 @@
             delta_v[:, at] = jnp.sum(gf * o_t[:, at], axis=0, keepdims=True)
             dop[at, :] = (gf * l_v[:, at]).T.astype(bf16)
 
-    def grads_of(at_row, size, ds, col):
+    def value_grads(at_row, size):
+        return dot(p_v[pl.ds(at_row, size), :], dop[...])
+
+    def key_grads(at_row, size, ds, col):
         here = pl.ds(at_row, size)
         vblk = vb[here, :]
         for c in range(ROWS // 256):
             at = pl.ds(c * 256, 256)
             dp = dot(vblk, dot_t[:, at])
             ds[:, pl.ds(col + c * 256, 256)] = (p_v[here, at].astype(f32) * (dp - delta_v[:, at])).astype(bf16)
-        dk = dot(ds[:, pl.ds(col, ROWS)], qp[...])
-        dv = dot(p_v[here, :], dop[...])
-        return dk, dv
+        return dot(ds[:, pl.ds(col, ROWS)], qp[...])
 
     row_terms(0)
     for c in (pair_relay[0], pair_relay[1], last_relay[0], last_relay[1]):
@@ -342,44 +343,71 @@
     project(1, 1)
     row_terms(1)
 
-    def core_copy(n):
-        return remote(csend.at[n], crecv.at[n], cs_sem.at[n], cr_sem.at[n], core)
-
-    z_dest = (z2, zp, zm, z2, zp, zm, yhp)
-
-    def z_copy(j):
-        return remote(zs.at[j], zr.at[j], zs_sem.at[j], zr_sem.at[j], z_dest[j])
-
     def own_half(n):
         return pl.ds(pl.multiple_of(n * PAIR + BLK, BLK), BLK)
 
-    def finish(n, j, extras):
-        total = s_v[own_half(n), 0:2 * HD] + crecv[n].astype(f32)
-        for e in extras:
-            z_copy(e).wait_recv()
-            total = total + zr[e].astype(f32)
-        if j < 7:
-            zs[j] = total.astype(bf16)
-            z_copy(j).start()
-        else:
-            dkp_ref[...] = total[:, 0:HD].astype(bf16)
-            dvp_ref[...] = total[:, HD:2 * HD].astype(bf16)
-
+    z_dest = (z2, zp, zm, z2, zp, zm, yhp)
     extras_of = ((), (), (), (), (), (), (0, 1, 2), (3, 4, 5, 6))
 
+    class Sums:
+        def __init__(self, kind, col, out):
+            self.kind, self.col, self.out = kind, pl.ds(col, HD), out
+
+        def core(self, n):
+            k = self.kind
+            return remote(csend.at[k, n], crecv.at[k, n], cs_sem.at[k, n], cr_sem.at[k, n], core)
+
+        def z(self, j):
+            k = self.kind
+            return remote(zs.at[k, j], zr.at[k, j], zs_sem.at[k, j], zr_sem.at[k, j], z_dest[j])
+
+        def give(self, n, grads):
+            csend[self.kind, n] = grads[0:BLK].astype(bf16)
+            self.core(n).start()
+            s_v[own_half(n), self.col] = grads[BLK:]
+
+        def finish(self, j):
+            self.core(j).wait_recv()
+            total = s_v[own_half(j), self.col] + crecv[self.kind, j].astype(f32)
+            for e in extras_of[j]:
+                self.z(e).wait_recv()
+                total = total + zr[self.kind, e].astype(f32)
+            if j < 7:
+                zs[self.kind, j] = total.astype(bf16)
+                self.z(j).start()
+            else:
+                self.out[...] = total.astype(bf16)
+
+        def wait_send(self):
+            for n in range(PAIRS):
+                self.core(n).wait_send()
+            for j in range(7):
+                self.z(j).wait_send()
+
+    key_sums = Sums(0, 0, dkp_ref)
+    value_sums = Sums(1, HD, dvp_ref)
+
+    def value_step(n, carry):
+        value_sums.give(n, value_grads(pair_at(n), PAIR))
+        for j in range(6):
+            @pl.when(n == j + 2)
+            def _():
+                value_sums.finish(j)
+        return carry
+
+    lax.fori_loop(0, PAIRS, value_step, 0)
+
     def pair_grads(n, ds, col):
-        dk, dv = grads_of(pair_at(n), PAIR, ds, col)
-        csend[n, :, 0:HD] = dk[0:BLK].astype(bf16)
-        csend[n, :, HD:2 * HD] = dv[0:BLK].astype(bf16)
-        core_copy(n).start()
-        s_v[own_half(n), 0:HD] = dk[BLK:]
-        s_v[own_half(n), HD:2 * HD] = dv[BLK:]
+        key_sums.give(n, key_grads(pair_at(n), PAIR, ds, col))
 
         for j in range(6):
             @pl.when(n == j + 1)
             def _():
-                core_copy(j).wait_recv()
-                finish(j, j, extras_of[j])
+                key_sums.finish(j)
+
+        @pl.when(n == 4)
+        def _():
+            value_sums.finish(6)
 
     def first_step(n, carry):
         pair_grads(n, w_v.at[pl.ds(0, PAIR)], pl.multiple_of(n * ROWS, ROWS))
@@ -393,11 +421,10 @@
 
     lax.fori_loop(PAIRS // 2, PAIRS, second_step, 0)
 
-    dk, dv = grads_of(16 * BLK, BLK, ds_v.at[pl.ds(8 * BLK, BLK)], 0)
-    dvn_ref[...] = dv.astype(bf16)
+    dvn_ref[...] = value_grads(16 * BLK, BLK).astype(bf16)
+    dk = key_grads(16 * BLK, BLK, ds_v.at[pl.ds(8 * BLK, BLK)], 0)
     dkn_ref[...] = (dk * cos_v[...] - pltpu.roll(dk, HD // 2, 1) * sin_v[...]).astype(bf16)
-    core_copy(6).wait_recv()
-    finish(6, 6, extras_of[6])
+    key_sums.finish(6)
 
     def query_step(c, carry):
         at = pl.ds(pl.multiple_of(c * 256, 256), 256)
@@ -421,17 +448,15 @@
                 y = x * cos_v[ta, :] - pltpu.roll(x, HD // 2, 1) * sin_v[ta, :]
                 dq_ref[pl.ds(pl.multiple_of(h * SEQ + k * CHUNK, CHUNK), CHUNK), :] = y.astype(bf16)
 
-    core_copy(7).wait_recv()
-    finish(7, 7, extras_of[7])
+    value_sums.finish(7)
+    key_sums.finish(7)
 
     keys.wait_send()
     vals.wait_send()
     for c in do_own + do_relay + pair_relay + last_relay:
         c.wait_send()
-    for n in range(PAIRS):
-        core_copy(n).wait_send()
-    for j in range(7):
-        z_copy(j).wait_send()
+    key_sums.wait_send()
+    value_sums.wait_send()
 
 
 def hand_over(*refs):
@@ -481,10 +506,10 @@
             pltpu.VMEM((SEQ, HD), f32),
             pltpu.VMEM((9 * BLK, ROWS), bf16),
             pltpu.VMEM((2, HEADS * HD, HD), f32),
-            pltpu.VMEM((PAIRS, BLK, 2 * HD), bf16),
-            pltpu.VMEM((PAIRS, BLK, 2 * HD), bf16),
-            pltpu.VMEM((7, BLK, 2 * HD), bf16),
-            pltpu.VMEM((7, BLK, 2 * HD), bf16),
+            pltpu.VMEM((2, PAIRS, BLK, HD), bf16),
+            pltpu.VMEM((2, PAIRS, BLK, HD), bf16),
+            pltpu.VMEM((2, 7, BLK, HD), bf16),
+            pltpu.VMEM((2, 7, BLK, HD), bf16),
             dma((7,)),
             dma((8,)),
             dma((8,)),
@@ -494,10 +519,10 @@
             dma((16,)),
             dma((15,)),
             dma((15,)),
-            dma((8,)),
-            dma((8,)),
-            dma((7,)),
-            dma((7,)),
+            dma((2, 8)),
+            dma((2, 8)),
+            dma((2, 7)),
+            dma((2, 7)),
         ],
         compiler_params=pltpu.CompilerParams(
             collective_id=0, has_side_effects=True, vmem_limit_bytes=60 * 1024 * 1024

time: 59 us -> 61.4 us (1.041)
  Pallas kernels: 57.5 us -> 60 us
    pallas_call x1, Pallas kernels: 55.7 us -> 58.1 us  [local(): pl.pallas_call(kernel, out_shape=(jax.ShapeDtypeStruct((ROWS, HD), bf16),...]
where the time goes in v6:
time: 61.4 us; the launch traced here: 61.2 us
  Pallas kernels  60 us (98%)
  between operations  1.29 us (2%)
    pallas_call x1, Pallas kernels, local(): pl.pallas_call(kernel, out_shape=(jax.ShapeDtypeStruct((ROWS, HD), bf16),...  58.1 us
    pallas_call x1, Pallas kernels, local(): pl.pallas_call(hand_over, out_shape=tuple((jax.ShapeDtypeStruct(g.shape,...  1.86 us

profile of v6, /device:TPU:1, one launch (start us, length us, event | category | flops | bytes accessed | tf_op | source)
XLA Modules:
  0.0 61.2 jit_solution(8578941666612078916)
XLA Ops:
  1.3 58.1 %attention_backward.1 = (bf16[1280,128]{1,0:T(8,128)(2,1)}, bf16[256,128]{1,0:T(8,128)(2,1)}, bf16[256,128]{1,0:T(8,128)(2,1)}, bf16[256,128]{1,0:T(8,128)(2,1)}, bf16[256,128]{1,0:T(8,128)(2,1)}) custom-call(bf16[32,5120]{1,0:T(8,128)(2,1)} %bitcast.21, bf16[640,5120]{1,0:T(8,128)(2,1)} %bitcast.20, bf16[1280,128]{1,0:T(8,128)(2,1)} %bitcast.22, ...), custom_call_target="tpu_custom_call" | custom-call | tf_op jit(solution)/shard_map/attention_backward/pallas_call | solution.py:475
  59.4 1.9 %hand_over.1 = (bf16[1280,128]{1,0:T(8,128)(2,1)}, bf16[256,128]{1,0:T(8,128)(2,1)}, bf16[256,128]{1,0:T(8,128)(2,1)}, bf16[256,128]{1,0:T(8,128)(2,1)}, bf16[256,128]{1,0:T(8,128)(2,1)}) custom-call(bf16[1280,128]{1,0:T(8,128)(2,1)} %get-tuple-element.15.refs_0_, bf16[256,128]{1,0:T(8,128)(2,1)} %get-tuple-element.16.refs_1_, ...), custom_call_target="tpu_custom_call" | custom-call | tf_op jit(solution)/shard_map/hand_over/pallas_call | solution.py:542

commit v7 on v6

--- a/solution.py
+++ b/solution.py
@@ -121,7 +121,7 @@
 
     keys = Spread(kp_hbm, kb, ksend, krecv, kfw)
     vals = Spread(vp_hbm, vb, vsend, vrecv, vfw)
-    for c in keys.own[:1] + vals.own[:1] + keys.own[1:] + vals.own[1:]:
+    for c in keys.own:
         c.start()
 
     mid = WIDTH // 2
@@ -148,7 +148,7 @@
         remote(rows(4, lo, 16, col, mid), rows(7, lo, 16, col, mid), dsend.at[i], drecv.at[i], ylp)
         for i, col, lo in ((11, 0, 0), (12, 0, 16), (13, mid, 0), (14, mid, 16))
     ]
-    for c in do_own:
+    for c in do_own[1:]:
         c.start()
 
     def kof(dyl, dx):
@@ -171,6 +171,9 @@
             tile = jnp.concatenate(parts, axis=0)
             qt[:, pl.ds((p * HEADS + h) * HD, HD)] = tile.T.astype(bf16)
 
+    for c in do_own[:1] + vals.own:
+        c.start()
+
     tl = lax.broadcasted_iota(jnp.int32, (1, HD), 1)
 
     def tokens(p):
@@ -227,9 +230,6 @@
             keys.take(6)
             for c in keys.relay:
                 c.start()
-            vals.take(6)
-            for c in vals.relay:
-                c.start()
             do_own[1].wait_recv()
             do_relay[0].start()
             do_own[2].wait_recv()
@@ -237,12 +237,13 @@
             for j in (5, 4, 3):
                 keys.take(j)
 
-        for j, ahead in ((4, 2), (5, 1), (6, 0)):
-            @pl.when(i == j)
-            def _():
-                keys.take(ahead)
-
-        @pl.when(i == 6)
+        @pl.when(i == 3)
+        def _():
+            vals.take(6)
+            for c in vals.relay:
+                c.start()
+
+        @pl.when(i == 5)
         def _():
             do_own[0].wait_recv()
             for c in pair_relay:
@@ -253,6 +254,17 @@
             local[6].wait()
             project(0, 0)
             project(0, 1)
+            for c in do_relay:
+                c.wait_recv()
+            for c in last_relay:
+                c.start()
+            for j in (2, 1, 0):
+                keys.take(j)
+
+        @pl.when(i == 7)
+        def _():
+            for j in (5, 4, 3):
+                vals.take(j)
 
         keys.forward(n).wait_recv()
         scores_of(n)
@@ -283,22 +295,10 @@
     def output_step(i, carry):
         n = PAIRS - 1 - i
 
-        @pl.when(i == 0)
-        def _():
-            for j in (5, 4, 3):
-                vals.take(j)
-
         for j, ahead in ((3, 2), (4, 1), (5, 0)):
             @pl.when(i == j)
             def _():
                 vals.take(ahead)
-
-        @pl.when(i == 1)
-        def _():
-            for c in do_relay:
-                c.wait_recv()
-            for c in last_relay:
-                c.start()
 
         vals.forward(n).wait_recv()
         output_of(pair_at(n), PAIR)
@@ -325,13 +325,15 @@
     def value_grads(at_row, size):
         return dot(p_v[pl.ds(at_row, size), :], dop[...])
 
-    def key_grads(at_row, size, ds, col):
+    def score_grads(at_row, size, ds, col):
         here = pl.ds(at_row, size)
         vblk = vb[here, :]
         for c in range(ROWS // 256):
             at = pl.ds(c * 256, 256)
             dp = dot(vblk, dot_t[:, at])
             ds[:, pl.ds(col + c * 256, 256)] = (p_v[here, at].astype(f32) * (dp - delta_v[:, at])).astype(bf16)
+
+    def key_grads(ds, col):
         return dot(ds[:, pl.ds(col, ROWS)], qp[...])
 
     row_terms(0)
@@ -387,42 +389,62 @@
     key_sums = Sums(0, 0, dkp_ref)
     value_sums = Sums(1, HD, dvp_ref)
 
-    def value_step(n, carry):
-        value_sums.give(n, value_grads(pair_at(n), PAIR))
+    VSTEP = 2
+
+    def value_step(i, carry):
+        grads = value_grads(pair_at(i * VSTEP), VSTEP * PAIR)
+        for j in range(VSTEP):
+            value_sums.give(i * VSTEP + j, grads[j * PAIR:(j + 1) * PAIR])
+        for j in range(6):
+            @pl.when(i == j // VSTEP + 1)
+            def _():
+                value_sums.finish(j)
+        return carry
+
+    lax.fori_loop(0, PAIRS // VSTEP, value_step, 0)
+
+    early = w_v.at[pl.ds(0, PAIR)]
+
+    def late(n):
+        return ds_v.at[pl.ds(pl.multiple_of((n - PAIRS // 2) * PAIR, PAIR), PAIR)]
+
+    def early_col(n):
+        return pl.multiple_of(n * ROWS, ROWS)
+
+    def send_on(n):
         for j in range(6):
             @pl.when(n == j + 2)
             def _():
-                value_sums.finish(j)
+                key_sums.finish(j)
+
+    def first_step(n, carry):
+        grads = key_grads(early, early_col(n - 1))
+        score_grads(pair_at(n), PAIR, early, early_col(n))
+        key_sums.give(n - 1, grads)
+        send_on(n)
         return carry
 
-    lax.fori_loop(0, PAIRS, value_step, 0)
-
-    def pair_grads(n, ds, col):
-        key_sums.give(n, key_grads(pair_at(n), PAIR, ds, col))
-
-        for j in range(6):
-            @pl.when(n == j + 1)
-            def _():
-                key_sums.finish(j)
-
-        @pl.when(n == 4)
-        def _():
-            value_sums.finish(6)
-
-    def first_step(n, carry):
-        pair_grads(n, w_v.at[pl.ds(0, PAIR)], pl.multiple_of(n * ROWS, ROWS))
+    def second_step(n, carry):
+        grads = key_grads(late(n - 1), 0)
+        score_grads(pair_at(n), PAIR, late(n), 0)
+        key_sums.give(n - 1, grads)
+        send_on(n)
         return carry
 
-    lax.fori_loop(0, PAIRS // 2, first_step, 0)
-
-    def second_step(n, carry):
-        pair_grads(n, ds_v.at[pl.ds(pl.multiple_of((n - PAIRS // 2) * PAIR, PAIR), PAIR)], 0)
-        return carry
-
-    lax.fori_loop(PAIRS // 2, PAIRS, second_step, 0)
+    score_grads(0, PAIR, early, 0)
+    lax.fori_loop(1, PAIRS // 2, first_step, 0)
+    grads = key_grads(early, (PAIRS // 2 - 1) * ROWS)
+    score_grads(PAIRS // 2 * PAIR, PAIR, late(PAIRS // 2), 0)
+    key_sums.give(PAIRS // 2 - 1, grads)
+    key_sums.finish(2)
+    value_sums.finish(6)
+    lax.fori_loop(PAIRS // 2 + 1, PAIRS, second_step, 0)
+    grads = key_grads(late(PAIRS - 1), 0)
+    score_grads(16 * BLK, BLK, ds_v.at[pl.ds(8 * BLK, BLK)], 0)
+    key_sums.give(PAIRS - 1, grads)
 
     dvn_ref[...] = value_grads(16 * BLK, BLK).astype(bf16)
-    dk = key_grads(16 * BLK, BLK, ds_v.at[pl.ds(8 * BLK, BLK)], 0)
+    dk = key_grads(ds_v.at[pl.ds(8 * BLK, BLK)], 0)
     dkn_ref[...] = (dk * cos_v[...] - pltpu.roll(dk, HD // 2, 1) * sin_v[...]).astype(bf16)
     key_sums.finish(6)
 

time: 61.4 us -> 57.6 us (0.938)
  Pallas kernels: 60 us -> 56.2 us
    pallas_call x1, Pallas kernels: 58.1 us -> 54.3 us  [local(): pl.pallas_call(kernel, out_shape=(jax.ShapeDtypeStruct((ROWS, HD), bf16),...]
where the time goes in v7:
time: 57.6 us; the launch traced here: 57.5 us
  Pallas kernels  56.2 us (98%)
  between operations  1.29 us (2%)
    pallas_call x1, Pallas kernels, local(): pl.pallas_call(kernel, out_shape=(jax.ShapeDtypeStruct((ROWS, HD), bf16),...  54.3 us
    pallas_call x1, Pallas kernels, local(): pl.pallas_call(hand_over, out_shape=tuple((jax.ShapeDtypeStruct(g.shape,...  1.86 us

profile of v7, /device:TPU:1, one launch (start us, length us, event | category | flops | bytes accessed | tf_op | source)
XLA Modules:
  0.0 57.5 jit_solution(4586098505593354396)
XLA Ops:
  1.3 54.3 %attention_backward.1 = (bf16[1280,128]{1,0:T(8,128)(2,1)}, bf16[256,128]{1,0:T(8,128)(2,1)}, bf16[256,128]{1,0:T(8,128)(2,1)}, bf16[256,128]{1,0:T(8,128)(2,1)}, bf16[256,128]{1,0:T(8,128)(2,1)}) custom-call(bf16[32,5120]{1,0:T(8,128)(2,1)} %bitcast.21, bf16[640,5120]{1,0:T(8,128)(2,1)} %bitcast.20, bf16[1280,128]{1,0:T(8,128)(2,1)} %bitcast.22, ...), custom_call_target="tpu_custom_call" | custom-call | tf_op jit(solution)/shard_map/attention_backward/pallas_call | solution.py:497
  55.6 1.9 %hand_over.1 = (bf16[1280,128]{1,0:T(8,128)(2,1)}, bf16[256,128]{1,0:T(8,128)(2,1)}, bf16[256,128]{1,0:T(8,128)(2,1)}, bf16[256,128]{1,0:T(8,128)(2,1)}, bf16[256,128]{1,0:T(8,128)(2,1)}) custom-call(bf16[1280,128]{1,0:T(8,128)(2,1)} %get-tuple-element.15.refs_0_, bf16[256,128]{1,0:T(8,128)(2,1)} %get-tuple-element.16.refs_1_, ...), custom_call_target="tpu_custom_call" | custom-call | tf_op jit(solution)/shard_map/hand_over/pallas_call | solution.py:564

commit v8 on v7

--- a/solution.py
+++ b/solution.py
@@ -17,6 +17,7 @@
 SEQ = 256
 HD = 128
 ROWS = HEADS * SEQ
+HALF = ROWS // 2
 BLK = 256
 WIDTH = 5120
 PROMPT = 4096
@@ -243,10 +244,17 @@
             for c in vals.relay:
                 c.start()
 
-        @pl.when(i == 5)
+        @pl.when(i == 4)
         def _():
             do_own[0].wait_recv()
             for c in pair_relay:
+                c.start()
+
+        @pl.when(i == 5)
+        def _():
+            for c in do_relay:
+                c.wait_recv()
+            for c in last_relay:
                 c.start()
             do_own[3].wait_recv()
             do_own[4].wait_recv()
@@ -254,10 +262,6 @@
             local[6].wait()
             project(0, 0)
             project(0, 1)
-            for c in do_relay:
-                c.wait_recv()
-            for c in last_relay:
-                c.start()
             for j in (2, 1, 0):
                 keys.take(j)
 
@@ -323,7 +327,8 @@
             dop[at, :] = (gf * l_v[:, at]).T.astype(bf16)
 
     def value_grads(at_row, size):
-        return dot(p_v[pl.ds(at_row, size), :], dop[...])
+        here = pl.ds(at_row, size)
+        return dot(p_v[here, HALF:], dop[HALF:, :]) + s_v[here, HD:2 * HD]
 
     def score_grads(at_row, size, ds, col):
         here = pl.ds(at_row, size)
@@ -337,6 +342,14 @@
         return dot(ds[:, pl.ds(col, ROWS)], qp[...])
 
     row_terms(0)
+
+    def first_value_step(i, carry):
+        here = pl.ds(pl.multiple_of(i * 2 * PAIR, 2 * PAIR), 2 * PAIR)
+        s_v[here, HD:2 * HD] = dot(p_v[here, 0:HALF], dop[0:HALF, :])
+        return carry
+
+    lax.fori_loop(0, PAIRS // 2, first_value_step, 0)
+    s_v[OWN, HD:2 * HD] = dot(p_v[OWN, 0:HALF], dop[0:HALF, :])
     for c in (pair_relay[0], pair_relay[1], last_relay[0], last_relay[1]):
         c.wait_recv()
     project(1, 0)

time: 57.6 us -> 59.4 us (1.031)
  Pallas kernels: 56.2 us -> 58 us
    pallas_call x1, Pallas kernels: 54.3 us -> 56.1 us  [local(): pl.pallas_call(kernel, out_shape=(jax.ShapeDtypeStruct((ROWS, HD), bf16),...]
where the time goes in v8:
time: 59.4 us; the launch traced here: 59.3 us
  Pallas kernels  58 us (98%)
  between operations  1.29 us (2%)
    pallas_call x1, Pallas kernels, local(): pl.pallas_call(kernel, out_shape=(jax.ShapeDtypeStruct((ROWS, HD), bf16),...  56.1 us
    pallas_call x1, Pallas kernels, local(): pl.pallas_call(hand_over, out_shape=tuple((jax.ShapeDtypeStruct(g.shape,...  1.86 us

profile of v8, /device:TPU:1, one launch (start us, length us, event | category | flops | bytes accessed | tf_op | source)
XLA Modules:
  0.0 59.3 jit_solution(14396518240942612648)
XLA Ops:
  1.3 56.1 %attention_backward.1 = (bf16[1280,128]{1,0:T(8,128)(2,1)}, bf16[256,128]{1,0:T(8,128)(2,1)}, bf16[256,128]{1,0:T(8,128)(2,1)}, bf16[256,128]{1,0:T(8,128)(2,1)}, bf16[256,128]{1,0:T(8,128)(2,1)}) custom-call(bf16[32,5120]{1,0:T(8,128)(2,1)} %bitcast.21, bf16[640,5120]{1,0:T(8,128)(2,1)} %bitcast.20, bf16[1280,128]{1,0:T(8,128)(2,1)} %bitcast.22, ...), custom_call_target="tpu_custom_call" | custom-call | tf_op jit(solution)/shard_map/attention_backward/pallas_call | solution.py:510
  57.4 1.9 %hand_over.1 = (bf16[1280,128]{1,0:T(8,128)(2,1)}, bf16[256,128]{1,0:T(8,128)(2,1)}, bf16[256,128]{1,0:T(8,128)(2,1)}, bf16[256,128]{1,0:T(8,128)(2,1)}, bf16[256,128]{1,0:T(8,128)(2,1)}) custom-call(bf16[1280,128]{1,0:T(8,128)(2,1)} %get-tuple-element.15.refs_0_, bf16[256,128]{1,0:T(8,128)(2,1)} %get-tuple-element.16.refs_1_, ...), custom_call_target="tpu_custom_call" | custom-call | tf_op jit(solution)/shard_map/hand_over/pallas_call | solution.py:577

commit v9 on v7

--- a/solution.py
+++ b/solution.py
@@ -237,7 +237,7 @@
             for j in (5, 4, 3):
                 keys.take(j)
 
-        @pl.when(i == 3)
+        @pl.when(i == 4)
         def _():
             vals.take(6)
             for c in vals.relay:

time: 57.6 us -> 57.1 us (level)
  Pallas kernels: 56.2 us -> 55.6 us
where the time goes in v9:
time: 57.1 us; the launch traced here: 56.9 us
  Pallas kernels  55.6 us (97%)
  between operations  1.29 us (2%)
    pallas_call x1, Pallas kernels, local(): pl.pallas_call(kernel, out_shape=(jax.ShapeDtypeStruct((ROWS, HD), bf16),...  53.8 us
    pallas_call x1, Pallas kernels, local(): pl.pallas_call(hand_over, out_shape=tuple((jax.ShapeDtypeStruct(g.shape,...  1.86 us

profile of v9, /device:TPU:1, one launch (start us, length us, event | category | flops | bytes accessed | tf_op | source)
XLA Modules:
  0.0 56.9 jit_solution(696468503763242226)
XLA Ops:
  1.3 53.8 %attention_backward.1 = (bf16[1280,128]{1,0:T(8,128)(2,1)}, bf16[256,128]{1,0:T(8,128)(2,1)}, bf16[256,128]{1,0:T(8,128)(2,1)}, bf16[256,128]{1,0:T(8,128)(2,1)}, bf16[256,128]{1,0:T(8,128)(2,1)}) custom-call(bf16[32,5120]{1,0:T(8,128)(2,1)} %bitcast.21, bf16[640,5120]{1,0:T(8,128)(2,1)} %bitcast.20, bf16[1280,128]{1,0:T(8,128)(2,1)} %bitcast.22, ...), custom_call_target="tpu_custom_call" | custom-call | tf_op jit(solution)/shard_map/attention_backward/pallas_call | solution.py:497
  55.1 1.9 %hand_over.1 = (bf16[1280,128]{1,0:T(8,128)(2,1)}, bf16[256,128]{1,0:T(8,128)(2,1)}, bf16[256,128]{1,0:T(8,128)(2,1)}, bf16[256,128]{1,0:T(8,128)(2,1)}, bf16[256,128]{1,0:T(8,128)(2,1)}) custom-call(bf16[1280,128]{1,0:T(8,128)(2,1)} %get-tuple-element.15.refs_0_, bf16[256,128]{1,0:T(8,128)(2,1)} %get-tuple-element.16.refs_1_, ...), custom_call_target="tpu_custom_call" | custom-call | tf_op jit(solution)/shard_map/hand_over/pallas_call | solution.py:564
